TPU v7x, 32 devices: a whole 2x2x4 slice. The times are simulated.
32 devices in a mesh: replica: 8 (over z, core), tensor: 4 (over y, x).
Axes of the slice: x: 2, y: 2, z: 4, core: 2. Of those that a mesh axis runs over, the one named last changes fastest.
Arguments:
- x_input: bfloat16 [2048, 4096], P('replica', 'tensor'), may hold values from -6 to 6
- z_input: bfloat16 [2048, 4096], P('replica', 'tensor'), may hold values from -6 to 6
- bc_input: bfloat16 [2048, 1024], P('replica'), may hold values from -6 to 6
- dt_raw: float32 [2048, 128], P('replica', 'tensor'), may hold values from -6 to 6
- dt_bias: float32 [128], P('tensor'), may hold values from -3 to -1
- decay_rates: float32 [128], P('tensor'), may hold values from 0.005 to 0.5
- skip_gain: float32 [128], P('tensor'), may hold values from 0.5 to 1.5
- conv_x: float32 [4, 4096], P(None, 'tensor'), may hold values from -3 to 3
- conv_bc: float32 [4, 1024], replicated, may hold values from -3 to 3
- norm_gain: float32 [4096], P('tensor'), may hold values from 0.5 to 1.5
- out_weight: bfloat16 [4096, 4096], P('tensor'), may hold values from -0.09375 to 0.09375
- cached_states: float32 [16, 128, 32, 128], P('replica', 'tensor'), may hold values from -4 to 4
- cached_tail_x: float32 [16, 3, 4096], P('replica', None, 'tensor'), may hold values from -6 to 6
- cached_tail_bc: float32 [16, 3, 1024], P('replica'), may hold values from -6 to 6
- prefix_block: int32 [16], replicated, may hold values from 0 to 15, as said below
- lengths: int32 [16], P('replica'), may hold values from 128 to 128, as said below
Outputs:
- mixed: bfloat16 [2048, 4096], P(('replica', 'tensor'))
- final_states: float32 [16, 128, 32, 128], P('replica', 'tensor')
Inputs may be any that keep to these rules, and one draw needn't show every extreme that they name: A permutation: request q (on replica q // 2) starts from cached block prefix_block[q], which replica prefix_block[q] // 2 holds; every cached block feeds exactly one request. `lengths`: every request's suffix fills all 128 of its slots, so every entry is 128.
All inputs are finite; a program needn't handle non-finite values.
Results may differ from a plain program's by a relative error of at most 0.015.
Values may be sent and summed in bfloat16 or wider, within the bound.
No kernel may reach another device: no remote copies, remote signals or barrier semaphores. Data moves between devices by JAX's collectives and lax.ppermute only.
A program may use at most 64 MiB of HBM per device.

v0:
```python
import math
from functools import partial

import jax
import jax.numpy as jnp
from jax import lax
from jax.experimental import pallas as pl
from jax.experimental.pallas import tpu as pltpu
from jax.sharding import PartitionSpec as P

HEADS = 128
HEAD_DIM = 32
STATE = 128
GROUPS = 4
CONV = 4


highest = lax.Precision.HIGHEST
epsilon = 1e-05
f32 = jnp.float32
bf16 = jnp.bfloat16
LOG2E = math.log2(math.e)
MIB = 1024 * 1024
VMEM_LIMIT = 24


def causal_conv(tail_rows, sequence, kernel):
    joined = jnp.concatenate([tail_rows, sequence], axis=0)
    length = sequence.shape[0]
    total = joined[0:length] * kernel[0][None, :]
    for offset in range(1, kernel.shape[0]):
        total = total + joined[offset : offset + length] * kernel[offset][None, :]
    return jax.nn.silu(total)


def span_scan(inputs, b_heads, c_heads, step_sizes, decay_rates, skip_gain, carry_state):
    logdec = -step_sizes * decay_rates[None, :]
    cumulative = jnp.cumsum(logdec, axis=0)
    count_rows = inputs.shape[0]
    causal = jnp.arange(count_rows)[:, None] >= jnp.arange(count_rows)[None, :]
    cum_heads = jnp.transpose(cumulative)
    differ = cum_heads[:, :, None] - cum_heads[:, None, :]
    decays = jnp.where(causal[None, :, :], jnp.exp(jnp.minimum(differ, 0.0)), 0.0)
    scores = jnp.einsum("ihn,jhn->hij", c_heads, b_heads, precision=highest)
    weights = scores * decays * jnp.transpose(step_sizes)[:, None, :]
    inside = jnp.einsum("hij,jhp->ihp", weights, inputs, precision=highest)
    carried = jnp.exp(cumulative)[:, :, None] * jnp.einsum(
        "ihn,hpn->ihp", c_heads, carry_state, precision=highest
    )
    output = inside + carried + skip_gain[None, :, None] * inputs
    ending = cumulative[-1]
    weigh_in = jnp.exp(ending[None, :] - cumulative) * step_sizes
    new_state = jnp.exp(ending)[:, None, None] * carry_state + jnp.einsum(
        "jh,jhp,jhn->hpn", weigh_in, inputs, b_heads, precision=highest
    )
    return (output, new_state)


def local_any(
    x_input,
    z_input,
    bc_input,
    dt_raw,
    dt_bias,
    decay_rates,
    skip_gain,
    conv_x,
    conv_bc,
    norm_gain,
    out_weight,
    cached_states,
    cached_tail_x,
    cached_tail_bc,
    prefix_block,
    lengths,
):
    requests = lengths.shape[0]
    local_heads = dt_raw.shape[1]
    tokens_dev = x_input.shape[0]
    slot_len = tokens_dev // requests
    wanted = lax.dynamic_slice_in_dim(prefix_block, lax.axis_index("replica") * requests, requests)

    def migrate(rows):
        rows = lax.all_gather(rows.astype(bf16), "replica", axis=0, tiled=True)
        return jnp.take(rows, wanted, axis=0).astype(f32)

    start_states = migrate(cached_states)
    start_tail_x = migrate(cached_tail_x)
    start_tail_bc = migrate(cached_tail_bc)
    head_ids = lax.axis_index("tensor") * local_heads + jnp.arange(local_heads)
    member = ((head_ids // (HEADS // GROUPS))[:, None] == jnp.arange(GROUPS)[None, :]).astype(f32)
    live = jnp.arange(slot_len)[None, :] < lengths[:, None]
    outputs = []
    finals = []
    for request in range(requests):
        row_lo = request * slot_len
        row_hi = row_lo + slot_len
        inputs = causal_conv(
            start_tail_x[request], x_input[row_lo:row_hi].astype(f32), conv_x
        ).reshape(slot_len, local_heads, HEAD_DIM)
        bc_conv = causal_conv(
            start_tail_bc[request], bc_input[row_lo:row_hi].astype(f32), conv_bc
        )
        b_groups = bc_conv[:, : GROUPS * STATE].reshape(slot_len, GROUPS, STATE)
        c_groups = bc_conv[:, GROUPS * STATE :].reshape(slot_len, GROUPS, STATE)
        b_heads = jnp.einsum("lgn,hg->lhn", b_groups, member, precision=highest)
        c_heads = jnp.einsum("lgn,hg->lhn", c_groups, member, precision=highest)
        step_sizes = jnp.where(
            live[request][:, None], jax.nn.softplus(dt_raw[row_lo:row_hi] + dt_bias[None, :]), 0.0
        )
        output, carry_state = span_scan(
            inputs, b_heads, c_heads, step_sizes, decay_rates, skip_gain, start_states[request]
        )
        outputs.append(output.reshape(slot_len, -1))
        finals.append(carry_state)
    outputs = jnp.concatenate(outputs, axis=0)
    final_states = jnp.stack(finals, axis=0)
    gate_vals = outputs * jax.nn.silu(z_input.astype(f32))
    by_head = gate_vals.reshape(tokens_dev, local_heads, HEAD_DIM)
    head_squares = jnp.sum(by_head * by_head, axis=2)
    partial_sq = jnp.dot(head_squares, member, precision=highest)
    totals = lax.psum(partial_sq, "tensor")
    mean_sq = jnp.dot(totals, jnp.transpose(member), precision=highest) / (
        HEADS * HEAD_DIM // GROUPS
    )
    normed = (by_head * lax.rsqrt(mean_sq + epsilon)[:, :, None]).reshape(
        tokens_dev, -1
    ) * norm_gain[None, :]
    gated = jnp.where(live.reshape(tokens_dev, 1), normed, 0.0).astype(bf16)
    mixed = lax.psum_scatter(
        jnp.dot(gated, out_weight, preferred_element_type=f32).astype(bf16),
        "tensor",
        scatter_dimension=0,
        tiled=True,
    )
    return (mixed, final_states)


CHIPS = 4
SLOTS = 2
ITEMS = 2 * SLOTS
ROWS = 1024
HALF = ROWS // 2
TAIL = 32
ITEM_ROWS = HALF + TAIL // 2
LANES = 128
COLUMN_BLOCKS = ROWS // LANES
WIDE = ROWS + 2 * STATE
EARLY = CONV - 1
BASE = (3, 2, 2)
EXTRAS = ((0, 0, 0), (0, 1, 0), (0, 0, 1), (1, 2, 2))
SEND_PLAN = 0
PLACE_PLAN = 3 * ITEMS
CHUNKS = ((0, 4), (4, 8))
TILE = 512

HBM = pl.BlockSpec(memory_space=pltpu.HBM)
ANYWHERE = pl.BlockSpec(memory_space=pl.ANY)
VMEM = pl.BlockSpec(memory_space=pltpu.VMEM)
SMEM = pl.BlockSpec(memory_space=pltpu.SMEM)


def sds(shape, dtype):
    return jax.ShapeDtypeStruct(shape, dtype)


def params():
    return pltpu.CompilerParams(vmem_limit_bytes=VMEM_LIMIT * MIB)


def in_hbm(value):
    return pltpu.with_memory_space_constraint(value, pltpu.HBM)


def cost(nbytes, flops=0):
    return pl.CostEstimate(flops=flops, bytes_accessed=nbytes, transcendentals=0)


def silu(value):
    half = 0.5 * value
    return half + half * jnp.tanh(half)


def chip_and_core():
    replica = lax.axis_index("replica")
    return replica // 2, lax.rem(replica, 2)


def half_at(core):
    return pl.ds(pl.multiple_of(core * HALF, HALF), HALF)


def tail_half(core):
    return pl.ds(pl.multiple_of(core * (TAIL // 2), TAIL // 2), TAIL // 2)


def pack_kernel(
    prefix,
    states,
    tail_x,
    tail_bc,
    send,
    keep,
    plan,
    variant,
    blocks,
    rows_x,
    rows_bc,
    scratch,
    sems,
):
    _, core = chip_and_core()
    group = lax.axis_index("tensor")
    copies = [
        pltpu.make_async_copy(states.at[:, half_at(1 - core)], blocks.at[0], sems.at[0]),
        pltpu.make_async_copy(tail_x, rows_x, sems.at[1]),
        pltpu.make_async_copy(tail_bc, rows_bc, sems.at[2]),
        pltpu.make_async_copy(states.at[:, half_at(core)], blocks.at[1], sems.at[3]),
    ]
    for copy in copies:
        copy.start()
    make_plan(prefix, plan, variant)
    for copy in copies:
        copy.wait()
    scratch[...] = jnp.zeros_like(scratch)
    for block in range(SLOTS):
        for k in range(CONV - 1):
            for s in range(COLUMN_BLOCKS):
                scratch[3 * s + k : 3 * s + k + 1, :] = rows_x[
                    k, block : block + 1, s * LANES : (s + 1) * LANES
                ]
            for s in range(2):
                at = pl.multiple_of((s * GROUPS + group) * STATE, STATE)
                row = 3 * (COLUMN_BLOCKS + s) + k
                scratch[row : row + 1, :] = rows_bc[k, block : block + 1, pl.ds(at, STATE)]
        for part, out in enumerate((send, keep)):
            half = jnp.bitwise_xor(core, 1 - part)
            out[block, :HALF, :] = blocks[part, block].astype(bf16)
            out[block, HALF:, :] = scratch[tail_half(half), :].astype(bf16)


def make_plan(prefix, plan, variant):
    chip, core = chip_and_core()
    need = [jnp.int32(0)] * CHIPS
    for entry in range(PLACE_PLAN):
        plan[SEND_PLAN + entry] = 0
    for target in range(CHIPS):
        blocks = [prefix[target * ITEMS + place] for place in range(ITEMS)]
        sources = [block // ITEMS for block in blocks]
        for place in range(ITEMS):
            source = sources[place]
            item = lax.rem(blocks[place], ITEMS)
            rank = jnp.int32(0)
            for other in range(place):
                rank += jnp.where(sources[other] == source, 1, 0)
            distance = jnp.bitwise_xor(source, target)
            for d in range(1, CHIPS):
                need[d] = jnp.where(distance == d, jnp.maximum(need[d], rank + 1), need[d])

            @pl.when((source == chip) & (distance > 0))
            def _():
                plan[SEND_PLAN + (distance - 1) * ITEMS + rank] = item

            @pl.when(target == chip)
            def _():
                owner = jnp.bitwise_xor(core, place // SLOTS)
                at = PLACE_PLAN + owner * SLOTS + place % SLOTS
                plan[at] = distance * ITEMS + jnp.where(distance == 0, item, rank)

    choice = jnp.int32(len(EXTRAS) - 1)
    for v in reversed(range(len(EXTRAS) - 1)):
        fits = need[1] <= BASE[0] + EXTRAS[v][0]
        for d in range(2, CHIPS):
            fits = fits & (need[d] <= BASE[d - 1] + EXTRAS[v][d - 1])
        choice = jnp.where(fits, v, choice)
    variant[0] = choice


def copy_item(out, at, keep, recv, item, core):
    slot = lax.rem(item, SLOTS)
    mine = item // SLOTS == core

    @pl.when(mine)
    def _():
        out[at] = keep[slot]

    @pl.when(jnp.logical_not(mine))
    def _():
        out[at] = recv[slot]


def select_kernel(first, counts, plan, keep, recv, *outs):
    _, core = chip_and_core()
    outs = iter(outs)
    for d in range(1, CHIPS):
        if counts[d - 1]:
            out = next(outs)
            for slot in range(counts[d - 1]):
                item = plan[SEND_PLAN + (d - 1) * ITEMS + first[d - 1] + slot]
                copy_item(out, slot, keep, recv, item, core)


def spread_kernel(counts, *refs):
    outs = refs[-(CHIPS - 1) :]
    came = iter(refs)
    for n, out in zip(counts, outs):
        if n:
            out[:n] = next(came)[...]


def place_kernel(plan, _, keep, recv, *refs):
    came, (mine, other) = refs[: 2 * (CHIPS - 1)], refs[-2:]
    _, core = chip_and_core()
    for o, out in enumerate((other, mine)):
        for slot in range(SLOTS):
            code = plan[PLACE_PLAN + (1 - o) * SLOTS + slot]
            d = code // ITEMS
            which = lax.rem(code, ITEMS)

            @pl.when(d == 0)
            def _():
                copy_item(out, slot, keep, recv, which, core)

            for e in range(1, CHIPS):
                few = BASE[e - 1]
                base, extra = came[e - 1], came[e + 2]

                @pl.when((d == e) & (which < few))
                def _():
                    out[slot] = base[jnp.minimum(which, few - 1)]

                @pl.when((d == e) & (which >= few))
                def _():
                    out[slot] = extra[jnp.maximum(which - few, 0)]


def scan_kernel(
    _,
    lengths,
    x_in,
    z_in,
    bc_in,
    dt_raw,
    dt_bias,
    decay,
    skip,
    conv_x,
    conv_bc,
    weight,
    y_in,
    y_scale,
    c_out,
    s_add,
    s_scale,
    e_scale,
    early,
    staged,
    u,
    sems,
):
    parts = sems.shape[0]
    deep = weight.shape[0] // parts
    copies = []
    for i in range(parts):
        at = slice(i * deep, (i + 1) * deep)
        copies.append(pltpu.make_async_copy(weight.at[at], staged.at[at], sems.at[i]))
        copies[-1].start()
    group = lax.axis_index("tensor")
    span = x_in.shape[0] // SLOTS
    heads = dt_raw.shape[0]
    row = lax.broadcasted_iota(jnp.int32, (span, span), 0)
    column = lax.broadcasted_iota(jnp.int32, (span, span), 1)
    causal = row >= column
    lower = causal.astype(f32)
    late = causal & (column >= EARLY)
    head_row = lax.broadcasted_iota(jnp.int32, (heads, ROWS), 0)
    head_column = lax.broadcasted_iota(jnp.int32, (heads, ROWS), 1) // HEAD_DIM
    expand = (head_row == head_column).astype(f32)
    skip_wide = jnp.dot(skip[...], expand, precision=highest, preferred_element_type=f32)
    same = lax.broadcasted_iota(jnp.int32, (heads, heads), 0) == lax.broadcasted_iota(
        jnp.int32, (heads, heads), 1
    )

    def upright(value):
        return jnp.sum(jnp.where(same, value, 0.0), axis=1, keepdims=True)

    bias = upright(dt_bias[...])
    rate = upright(decay[...]) * (-LOG2E)
    per_block = LANES // HEAD_DIM
    lane_head = lax.broadcasted_iota(jnp.int32, (span, LANES), 1) // HEAD_DIM
    token = lax.broadcasted_iota(jnp.int32, (heads, span), 1)
    over_last = (((1,), (1,)), ((), ()))
    over_first = (((0,), (0,)), ((), ()))
    u[0:8, :] = jnp.zeros((8, WIDE), f32)
    for r in range(SLOTS):
        rows = slice(r * span, (r + 1) * span)
        u[8 : 8 + span, :ROWS] = x_in[rows, :].astype(f32)
        for s in range(2):
            at = pl.multiple_of((s * GROUPS + group) * STATE, STATE)
            lo = ROWS + s * STATE
            u[8 : 8 + span, lo : lo + STATE] = bc_in[rows, pl.ds(at, STATE)].astype(f32)

        def conv(lo, taps):
            at = slice(lo, lo + LANES)
            total = u[5 : 5 + span, at] * taps(0)
            early[r, 1, 0:1, at] = taps(0)
            for k in range(1, CONV):
                total = total + u[5 + k : 5 + k + span, at] * taps(k)
                early[r, 1, k : k + 1, at] = taps(k)
            early[r, 0, :, at] = total[:8]
            return silu(total)

        def bc_conv(s):
            at = pl.multiple_of((s * GROUPS + group) * STATE, STATE)
            return conv(ROWS + s * STATE, lambda k: conv_bc[k : k + 1, pl.ds(at, STATE)])

        b_mat = bc_conv(0).astype(bf16)
        c_mat = bc_conv(1).astype(bf16)
        c_out[rows, :] = c_mat
        scores = lax.dot_general(c_mat, b_mat, over_last, preferred_element_type=f32)
        scores = jnp.where(late, scores, 0.0)

        raw = dt_raw[:, rows] + bias
        steps = jnp.maximum(raw, 0.0) + jnp.log1p(jnp.exp(-jnp.abs(raw)))
        steps = jnp.where(token < lengths[r], steps, 0.0)
        logdec = steps * rate
        cum = lax.dot_general(
            lower, logdec, over_last, precision=highest, preferred_element_type=f32
        )
        cum_t = lax.dot_general(
            logdec, lower, over_last, precision=highest, preferred_element_type=f32
        )
        begin = cum_t[:, EARLY - 1 : EARLY]
        ending = cum_t[:, span - 1 : span]
        s_scale[r] = jnp.broadcast_to(jnp.exp2(ending - begin), (heads, LANES))
        e_scale[r] = jnp.broadcast_to(jnp.exp2(begin), (heads, LANES))
        weigh = jnp.where(token >= EARLY, jnp.exp2(ending - cum_t) * steps, 0.0)
        since = jnp.exp2(jnp.minimum(cum_t - begin, 0.0))
        wide = lax.dot_general(
            jnp.concatenate([steps, weigh, since, cum_t], axis=1),
            expand,
            over_first,
            precision=highest,
            preferred_element_type=f32,
        )
        early[r, 2, :, :ROWS] = wide[:8]
        early[r, 3, :, :ROWS] = wide[3 * span : 3 * span + 8]
        early[r, 5, :, :ROWS] = jnp.broadcast_to(skip_wide, (8, ROWS))
        for q in range(COLUMN_BLOCKS):
            lo = q * LANES
            cols = slice(lo, lo + LANES)
            xc = conv(lo, lambda k: conv_x[k : k + 1, cols])
            xdt = (xc * wide[:span, cols]).astype(bf16)
            xw = (xc * wide[span : 2 * span, cols]).astype(bf16)
            s_add[r, lo : lo + LANES, :] = lax.dot_general(
                xw, b_mat, over_first, preferred_element_type=f32
            )
            total = skip_wide[:, cols] * xc
            parts = []
            masked = []
            for i in range(per_block):
                h = q * per_block + i
                differ = cum[:, h : h + 1] - cum_t[h : h + 1, :]
                parts.append((jnp.exp2(jnp.minimum(differ, 0.0)) * scores).astype(bf16))
                masked.append(jnp.where(lane_head == i, xdt, jnp.zeros_like(xdt)))
            total = total + jnp.dot(
                jnp.concatenate(parts, axis=1),
                jnp.concatenate(masked, axis=0),
                preferred_element_type=f32,
            )
            gate = silu(z_in[rows, cols].astype(f32))
            early[r, 4, :, cols] = gate[:8]
            y_in[rows, cols] = total * gate
            y_scale[rows, cols] = wide[2 * span : 3 * span, cols] * gate
    for copy in copies:
        copy.wait()


def by_head(state, scale):
    heads = scale.shape[0]
    wide = state.astype(f32).reshape(heads, HEAD_DIM, LANES) * scale[:, None, :]
    return wide.reshape(heads * HEAD_DIM, LANES)


def first_tokens(early, tails):
    row = lax.broadcasted_iota(jnp.int32, (8, WIDE), 0)
    taps = early[1]
    tail = tails[...]
    total = early[0]
    for t in range(EARLY):
        add = sum(taps[k : k + 1] * tail[t + k : t + k + 1] for k in range(EARLY - t))
        total = jnp.where(row == t, total + add, total)
    act = silu(total)
    return act[:, :ROWS], act[:, ROWS : ROWS + STATE], act[:, ROWS + STATE :]


def gate_rows(
    lengths,
    y_in,
    y_scale,
    c_in,
    e_scale,
    early,
    mine,
    other,
    gain,
    gated,
    x_first,
    b_first,
    start,
    tails,
    tail_rows,
):
    _, core = chip_and_core()
    tensor = lax.axis_index("tensor")
    x, y = lax.rem(tensor, 2), tensor // 2
    tokens = y_in.shape[0]
    span = tokens // SLOTS
    quarter = tokens // 4
    over_last = (((1,), (1,)), ((), ()))
    over_first = (((0,), (0,)), ((), ()))
    row = lax.broadcasted_iota(jnp.int32, (8, ROWS), 0)
    tail_rows[...] = jnp.zeros_like(tail_rows)
    for r in range(SLOTS):
        rows = slice(r * span, (r + 1) * span)
        start[half_at(core), :] = mine[r, :HALF]
        start[half_at(1 - core), :] = other[r, :HALF]
        tails[tail_half(core), :] = mine[r, HALF:].astype(f32)
        tails[tail_half(1 - core), :] = other[r, HALF:].astype(f32)
        for s in range(COLUMN_BLOCKS + 2):
            tail_rows[:EARLY, s * LANES : (s + 1) * LANES] = tails[3 * s : 3 * s + 3, :]

        x_8, b_8, c_8 = first_tokens(early[r], tail_rows)
        steps, cum, gate_8 = early[r, 2, :, :ROWS], early[r, 3, :, :ROWS], early[r, 4, :, :ROWS]
        skip = early[r, 5, 0:1, :ROWS]
        moved = steps * x_8
        last = cum[EARLY - 1 : EARLY]
        kept = jnp.where(row < EARLY, jnp.exp2(jnp.minimum(last - cum, 0.0)) * moved, 0.0)
        x_first[r] = kept
        b_first[r] = b_8
        after = by_head(start[...], e_scale[r]) + lax.dot_general(
            kept, b_8, over_first, preferred_element_type=f32
        )
        y_8 = skip * x_8 + jnp.exp2(cum) * lax.dot_general(
            c_8.astype(bf16), start[...], over_last, preferred_element_type=f32
        )
        scores = lax.dot_general(c_8, b_8, over_last, preferred_element_type=f32)
        for j in range(EARLY):
            decay = jnp.exp2(jnp.minimum(cum - cum[j : j + 1], 0.0))
            y_8 += jnp.where(row >= j, scores[:, j : j + 1] * decay * moved[j : j + 1], 0.0)

        carried = lax.dot_general(
            c_in[rows, :], after.astype(bf16), over_last, preferred_element_type=f32
        )
        value = y_in[rows, :] + y_scale[rows, :] * carried
        value = jnp.concatenate([jnp.where(row < EARLY, y_8 * gate_8, value[:8]), value[8:]], axis=0)
        mean_sq = jnp.mean(value * value, axis=1, keepdims=True)
        live = lax.broadcasted_iota(jnp.int32, (span, 1), 0) < lengths[r]
        scale = jnp.where(live, lax.rsqrt(mean_sq + epsilon), 0.0)
        result = (value * scale * gain[...]).astype(bf16)
        for part in range(span // quarter):
            owner = r * (span // quarter) + part
            place = jnp.bitwise_xor(owner // 2, y) + 2 * jnp.bitwise_xor(owner % 2, x)
            at = pl.ds(pl.multiple_of(place * quarter, quarter), quarter)
            gated[at, :] = result[part * quarter : (part + 1) * quarter, :]


def project_kernel(first, columns, *refs):
    if first:
        *ins, weight, gated, x_first, b_first = refs[:13]
        l_send, l_own, l_on, r_send, r_own, r_on, *scratch = refs[13:]
        gate_rows(*ins, gated, x_first, b_first, *scratch)
    else:
        gated, weight, l_send, l_own, l_on, r_send, r_own, r_on = refs
    q = gated.shape[0] // 4
    half = l_own.shape[1]
    tile = min(half, TILE)
    for lo in range(0, 2 * half, tile):
        at = slice(columns + lo, columns + lo + tile)
        product = jnp.dot(gated[...], weight[:, at], preferred_element_type=f32).astype(bf16)
        own, block_y, block_x, block_xy = (product[j * q : (j + 1) * q] for j in range(4))
        if lo < half:
            to = slice(lo, lo + tile)
            l_send[0, :, to] = block_x
            l_send[1, :, to] = block_xy
            l_own[:, to] = own
            l_on[:, to] = block_y
        else:
            to = slice(lo - half, lo - half + tile)
            r_send[0, :, to] = block_y
            r_send[1, :, to] = block_xy
            r_own[:, to] = own
            r_on[:, to] = block_x


def final_kernel(mine, other, x_first, b_first, s_add, s_scale, e_scale, out):
    _, core = chip_and_core()
    heads = s_scale.shape[1] // 2

    def put(half, piece):
        at = half_at(half)
        of = pl.ds(pl.multiple_of(half * heads, heads), heads)
        after = by_head(piece[0, :HALF], e_scale[0, of, :]) + lax.dot_general(
            x_first[0, :, at], b_first[0], (((0,), (0,)), ((), ())), preferred_element_type=f32
        )
        out[0, at, :] = by_head(after, s_scale[0, of, :]) + s_add[0, at, :]

    put(core, mine)
    put(1 - core, other)


def over_replica(value, bits):
    pairs = [(r, r ^ bits) for r in range(2 * CHIPS)]
    return lax.ppermute(value, "replica", pairs)


def over_tensor(value, bits):
    return lax.ppermute(value, "tensor", [(t, t ^ bits) for t in range(4)])


def select(first, counts, plan, keep, recv):
    with jax.named_scope("select"):
        return pl.pallas_call(
            partial(select_kernel, first, counts),
            out_shape=[sds((n, ITEM_ROWS, LANES), bf16) for n in counts if n],
            in_specs=[SMEM, VMEM, VMEM],
            out_specs=[VMEM for n in counts if n],
            compiler_params=params(),
        )(plan, keep, recv)


def exchange(counts, sends):
    bits = [2 * d for d in range(1, CHIPS) if counts[d - 1]]
    return [over_replica(value, b) for value, b in zip(sends, bits)]


def migrate_more(counts, plan, keep, recv):
    came = exchange(counts, select(BASE, counts, plan, keep, recv)) if any(counts) else []
    return pl.pallas_call(
        partial(spread_kernel, counts),
        out_shape=tuple(sds((n, ITEM_ROWS, LANES), bf16) for n in EXTRAS[-1]),
        in_specs=[VMEM] * len(came),
        out_specs=(VMEM,) * (CHIPS - 1),
        compiler_params=params(),
    )(*came)


def local_square(
    x_input,
    z_input,
    bc_input,
    dt_raw,
    dt_bias,
    decay_rates,
    skip_gain,
    conv_x,
    conv_bc,
    norm_gain,
    out_weight,
    cached_states,
    cached_tail_x,
    cached_tail_bc,
    prefix_block,
    lengths,
):
    tokens = x_input.shape[0]
    heads = dt_raw.shape[1]
    features = out_weight.shape[1]
    span = tokens // SLOTS

    with jax.named_scope("pack"):
        send, keep, plan, variant = pl.pallas_call(
            pack_kernel,
            out_shape=(sds((SLOTS, ITEM_ROWS, LANES), bf16),) * 2
            + (sds((PLACE_PLAN + ITEMS,), jnp.int32), sds((1,), jnp.int32)),
            in_specs=[SMEM, HBM, HBM, HBM],
            out_specs=(VMEM, VMEM, SMEM, SMEM),
            scratch_shapes=[
                pltpu.VMEM((2, SLOTS, HALF, LANES), f32),
                pltpu.VMEM((CONV - 1, SLOTS) + cached_tail_x.shape[2:], f32),
                pltpu.VMEM((CONV - 1, SLOTS) + cached_tail_bc.shape[2:], f32),
                pltpu.VMEM((TAIL, LANES), f32),
                pltpu.SemaphoreType.DMA((4,)),
            ],
            compiler_params=params(),
        )(
            prefix_block,
            in_hbm(cached_states.reshape(SLOTS, ROWS, LANES)),
            in_hbm(jnp.transpose(cached_tail_x, (1, 0, 2))),
            in_hbm(jnp.transpose(cached_tail_bc, (1, 0, 2))),
        )
    recv = over_replica(send, 1)
    more = lax.switch(
        variant.reshape(()),
        [partial(migrate_more, counts) for counts in EXTRAS],
        plan,
        keep,
        recv,
    )
    sends = select((0,) * (CHIPS - 1), BASE, plan, keep, recv)
    came = exchange(BASE, sends)

    with jax.named_scope("scan"):
        scale = sds((SLOTS, heads, LANES), f32)
        y_in, y_scale, c_mat, s_add, s_scale, e_scale, early, weight = pl.pallas_call(
            scan_kernel,
            out_shape=(
                sds((tokens, ROWS), f32),
                sds((tokens, ROWS), f32),
                sds((tokens, STATE), bf16),
                sds((SLOTS, ROWS, STATE), f32),
                scale,
                scale,
                sds((SLOTS, 6, 8, WIDE), f32),
                pltpu.VMEM(out_weight.shape, bf16),
            ),
            in_specs=[ANYWHERE, SMEM] + [VMEM] * 9 + [HBM],
            out_specs=(VMEM,) * 8,
            scratch_shapes=[pltpu.VMEM((8 + span, WIDE), f32), pltpu.SemaphoreType.DMA((4,))],
            compiler_params=params(),
            cost_estimate=cost(8 << 20, 1 << 30),
        )(
            sends[0],
            lengths,
            x_input,
            z_input,
            bc_input,
            jnp.transpose(dt_raw),
            dt_bias.reshape(1, heads),
            decay_rates.reshape(1, heads),
            skip_gain.reshape(1, heads),
            conv_x,
            conv_bc,
            in_hbm(out_weight),
        )

    with jax.named_scope("place"):
        mine, theirs = pl.pallas_call(
            place_kernel,
            out_shape=(sds((SLOTS, ITEM_ROWS, LANES), bf16),) * 2,
            in_specs=[SMEM, ANYWHERE] + [VMEM] * 8,
            out_specs=(VMEM, VMEM),
            compiler_params=params(),
        )(plan, c_mat, keep, recv, *came, *more)
    other = over_replica(theirs, 1)

    quarter = tokens // 4
    pieces = []
    gated = None
    for lo, hi in CHUNKS:
        lo, hi = lo * features // 8, hi * features // 8
        half = (hi - lo) // 2
        outs = [sds((2, quarter, half), bf16), sds((quarter, half), bf16), sds((quarter, half), bf16)]
        call = partial(
            pl.pallas_call,
            partial(project_kernel, gated is None, lo),
            compiler_params=params(),
            cost_estimate=cost(ROWS * (hi - lo) * 2, 2 * tokens * ROWS * (hi - lo)),
        )
        with jax.named_scope("project"):
            if gated is None:
                gated, x_first, b_first, *parts = call(
                    out_shape=[
                        sds((tokens, ROWS), bf16),
                        sds((SLOTS, 8, ROWS), f32),
                        sds((SLOTS, 8, STATE), f32),
                    ]
                    + 2 * outs,
                    in_specs=[SMEM] + [VMEM] * 9,
                    out_specs=[VMEM] * 9,
                    scratch_shapes=[
                        pltpu.VMEM((ROWS, LANES), bf16),
                        pltpu.VMEM((TAIL, LANES), f32),
                        pltpu.VMEM((8, WIDE), f32),
                    ],
                )(
                    lengths,
                    y_in,
                    y_scale,
                    c_mat,
                    e_scale,
                    early,
                    mine,
                    other,
                    norm_gain.reshape(1, ROWS),
                    weight,
                )
            else:
                parts = call(
                    out_shape=2 * outs,
                    in_specs=[VMEM, VMEM],
                    out_specs=[VMEM] * 6,
                )(gated, weight)
        pieces.append(parts)

    with jax.named_scope("final_states"):

        def of_request(*shape):
            return pl.BlockSpec((1,) + shape, lambda n: (n,) + (0,) * len(shape))

        final_states = pl.pallas_call(
            final_kernel,
            grid=(SLOTS,),
            out_shape=sds((SLOTS, ROWS, STATE), f32),
            in_specs=[
                of_request(ITEM_ROWS, LANES),
                of_request(ITEM_ROWS, LANES),
                of_request(8, ROWS),
                of_request(8, STATE),
                of_request(ROWS, STATE),
                of_request(heads, LANES),
                of_request(heads, LANES),
            ],
            out_specs=of_request(ROWS, STATE),
            compiler_params=params(),
            cost_estimate=cost(4 << 20),
        )(mine, other, x_first, b_first, s_add, s_scale, e_scale)

    with jax.named_scope("sum"):
        came = []
        for l_send, _, _, r_send, _, _ in pieces:
            came.append((over_tensor(l_send, 1), over_tensor(r_send, 2)))
        passed = []
        for (l_came, r_came), (_, l_own, l_on, _, r_own, r_on) in zip(came, pieces):
            onward = (l_on.astype(f32) + l_came[1].astype(f32)).astype(bf16)
            l_last = over_tensor(onward, 2)
            onward = (r_on.astype(f32) + r_came[1].astype(f32)).astype(bf16)
            r_last = over_tensor(onward, 1)
            passed.append(l_own.astype(f32) + l_came[0].astype(f32) + l_last.astype(f32))
            passed.append(r_own.astype(f32) + r_came[0].astype(f32) + r_last.astype(f32))
        mixed = jnp.concatenate(passed, axis=1).astype(bf16)

    return (mixed, final_states.reshape(cached_states.shape))


def solution(mesh):
    placed = (
        P("replica", "tensor"),
        P("replica", "tensor"),
        P("replica", None),
        P("replica", "tensor"),
        P("tensor"),
        P("tensor"),
        P("tensor"),
        P(None, "tensor"),
        P(),
        P("tensor"),
        P("tensor", None),
        P("replica", "tensor", None, None),
        P("replica", None, "tensor"),
        P("replica", None, None),
        P(),
        P("replica"),
    )
    square = mesh.shape["replica"] == 2 * CHIPS and mesh.shape["tensor"] == GROUPS
    return jax.shard_map(
        local_square if square else local_any,
        mesh=mesh,
        in_specs=placed,
        out_specs=(P(("replica", "tensor"), None), P("replica", "tensor", None, None)),
        check_vma=False,
    )
```

profile of v0, /device:TPU:8, one launch (start us, length us, event | category | flops | bytes accessed | tf_op | source)
XLA Modules:
  0.0 62.1 jit_solution(2945847465747958973)
XLA Ops:
  1.3 2.5 %pack.1 = (bf16[2,528,128]{2,1,0:T(8,128)(2,1)S(1)}, bf16[2,528,128]{2,1,0:T(8,128)(2,1)S(1)}, s32[16]{0:T(128)S(1)}, s32[1]{0:T(128)}) custom-call(s32[16]{0:T(128)S(1)} %copy-done.8, f32[2,1024,128]{2,1,0:T(8,128)} %bitcast.55, f32[3,2,1024]{2,1,0:T(2,128)} %bitcast.57, f32[3,2,1024]{2,1,0:T(2,128)} %bitcast.58), custom_call_target="tpu_custom_call" | custom-call | tf_op jit(solution)/shard_map/pack/pallas_call | solution.py:672
  3.9 1.5 %collective-permute-done.5.recv = bf16[2,528,128]{2,1,0:T(8,128)(2,1)S(1)} collective-permute-done((bf16[2,528,128]{2,1,0:T(8,128)(2,1)S(1)}, bf16[2,528,128]{2,1,0:T(8,128)(2,1)S(1)}, u32[]{:S(2)}, u32[]{:S(2)}) %collective-permute-start.5) | collective-permute-done | bytes 270368 | tf_op jit(solution)/shard_map/ppermute | solution.py:614
  6.9 3.1 %collective-permute-start.7 = (bf16[2,528,128]{2,1,0:T(8,128)(2,1)S(1)}, bf16[2,528,128]{2,1,0:T(8,128)(2,1)S(1)}, u32[]{:S(2)}, u32[]{:S(2)}) collective-permute-start(bf16[2,528,128]{2,1,0:T(8,128)(2,1)S(1)} %get-tuple-element.76), channel_id=1, source_target_pairs={{0,16},{4,20},{8,24},{12,28},{16,0},{20,4},{24,8},{28,12},{1,17},{... | collective-permute-start | bytes 811016 | tf_op jit(solution)/shard_map/ppermute | solution.py:614
  10.5 1.0 %copy-done = bf16[256,1024]{1,0:T(8,128)(2,1)S(1)} copy-done((bf16[256,1024]{1,0:T(8,128)(2,1)S(1)}, bf16[256,1024]{1,0:T(8,128)(2,1)}, u32[]{:S(2)}) %copy-start) | copy-done | bytes 524312
  11.5 1.0 %copy-done.1 = bf16[256,1024]{1,0:T(8,128)(2,1)S(1)} copy-done((bf16[256,1024]{1,0:T(8,128)(2,1)S(1)}, bf16[256,1024]{1,0:T(8,128)(2,1)}, u32[]{:S(2)}) %copy-start.1) | copy-done | bytes 524312
  12.5 1.0 %copy-done.2 = bf16[256,1024]{1,0:T(8,128)(2,1)S(1)} copy-done((bf16[256,1024]{1,0:T(8,128)(2,1)S(1)}, bf16[256,1024]{1,0:T(8,128)(2,1)}, u32[]{:S(2)}) %copy-start.2) | copy-done | bytes 524312
  18.4 8.8 %scan.1 = (f32[256,1024]{1,0:T(8,128)S(1)}, f32[256,1024]{1,0:T(8,128)S(1)}, bf16[256,128]{1,0:T(8,128)(2,1)S(1)}, f32[2,1024,128]{2,1,0:T(8,128)S(1)}, f32[2,32...) custom-call(bf16[3,528,128]{2,1,0:T(8,128)(2,1)S(1)} %get-tuple-elem, ...), custom_call_target="tpu_custom_call" | custom-call | flops 1073741824 | bytes 8388608 | tf_op jit(solution)/shard_map/scan/pallas_call | solution.py:705
  27.2 6.9 %collective-permute-done.8.refs_2_ = bf16[2,528,128]{2,1,0:T(8,128)(2,1)S(1)} collective-permute-done((bf16[2,528,128]{2,1,0:T(8,128)(2,1)S(1)}, bf16[2,528,128]{2,1,0:T(8,128)(2,1)S(1)}, u32[]{:S(2)}, u32[]{:S(2)}) %collective-permute-start.8) | collective-permute-done | bytes 270368 | tf_op jit(solution)/shard_map/ppermute | solution.py:614
  34.1 1.0 %place.1 = (bf16[2,528,128]{2,1,0:T(8,128)(2,1)S(1)}, bf16[2,528,128]{2,1,0:T(8,128)(2,1)S(1)}) custom-call(s32[16]{0:T(128)S(1)} %get-tuple-element.67.plan, bf16[256,128]{1,0:T(8,128)(2,1)S(1)} %get-tuple-element.73._.refs_3_, bf16[2,528,128]{2,1,0:T(8,128)(2,1)S(1)} %get-tuple-element.68.keep, bf16[2,528,128]{2,1,0:T(8,128)(2,1)S(1)} %collective-permute-done.5.recv, ...), custom_call_target="tpu_custom_call" | custom-call | tf_op jit(solution)/shard_map/place/pallas_call | solution.py:738
  35.2 1.5 %collective-permute-done.9.refs_7_.other = bf16[2,528,128]{2,1,0:T(8,128)(2,1)S(1)} collective-permute-done((bf16[2,528,128]{2,1,0:T(8,128)(2,1)S(1)}, bf16[2,528,128]{2,1,0:T(8,128)(2,1)S(1)}, u32[]{:S(2)}, u32[]{:S(2)}) %collective-permute-start.9) | collective-permute-done | bytes 270368 | tf_op jit(solution)/shard_map/ppermute | solution.py:614
  36.7 3.0 %project.2 = (bf16[256,1024]{1,0:T(8,128)(2,1)S(1)}, f32[2,8,1024]{2,1,0:T(8,128)S(1)}, f32[2,8,128]{2,1,0:T(8,128)S(1)}, bf16[2,64,1024]{2,1,0:T(8,128)(2,1)S(1...) custom-call(s32[2]{0:T(128)S(1)} %copy-done.7, ...), custom_call_target="tpu_custom_call" | custom-call | flops 1073741824 | bytes 4194304 | tf_op jit(solution)/shard_map/project/pallas_call | solution.py:762
  39.6 1.5 %collective-permute-start.10 = (bf16[2,64,1024]{2,1,0:T(8,128)(2,1)S(1)}, bf16[2,64,1024]{2,1,0:T(8,128)(2,1)S(1)}, u32[]{:S(2)}, u32[]{:S(2)}) collective-permute-start(bf16[2,64,1024]{2,1,0:T(8,128)(2,1)S(1)} %get-tuple-element.86), channel_id=1, source_target_pairs={{0,1},{1,0},{2,3},{3,2},{4,5},{5,4},{6,7},{7,6},{8,9},{9,8},{10,11... | collective-permute-start | bytes 786440 | tf_op jit(solution)/shard_map/sum/ppermute | solution.py:618
  41.2 1.5 %collective-permute-start.12 = (bf16[2,64,1024]{2,1,0:T(8,128)(2,1)S(1)}, bf16[2,64,1024]{2,1,0:T(8,128)(2,1)S(1)}, u32[]{:S(2)}, u32[]{:S(2)}) collective-permute-start(bf16[2,64,1024]{2,1,0:T(8,128)(2,1)S(1)} %get-tuple-element.89), channel_id=1, source_target_pairs={{0,2},{1,3},{2,0},{3,1},{4,6},{5,7},{6,4},{7,5},{8,10},{9,11},{10,... | collective-permute-start | bytes 786440 | tf_op jit(solution)/shard_map/sum/ppermute | solution.py:618
  42.7 1.3 %project.3 = (bf16[2,64,1024]{2,1,0:T(8,128)(2,1)S(1)}, bf16[64,1024]{1,0:T(8,128)(2,1)S(1)}, bf16[64,1024]{1,0:T(8,128)(2,1)S(1)}, bf16[2,64,1024]{2,1,0:T(8,12...) custom-call(bf16[256,1024]{1,0:T(8,128)(2,1)S(1)} %get-tuple-element.91.refs_0_, ...), custom_call_target="tpu_custom_call" | custom-call | flops 1073741824 | bytes 4194304 | tf_op jit(solution)/shard_map/project/pallas_call | solution.py:789
  45.1 1.5 %final_states.1 = f32[2,1024,128]{2,1,0:T(8,128)} custom-call(bf16[2,528,128]{2,1,0:T(8,128)(2,1)S(1)} %get-tuple-element.82.refs_6_.mine, bf16[2,528,128]{2,1,0:T(8,128)(2,1)S(1)} %collective-permute-done.9.refs_7_.other, f32[2,8,1024]{2,1,0:T(8,128)S(1)} %get-tuple-element.98.x_first, f32[2,8,128]{2,1,0:T(8,128)S(1)} %get-tuple-element.99.b_first, ...), custom_call_target="tpu_custom_call" | custom-call | bytes 4194304 | tf_op jit(solution)/shard_map/final_states/pallas_call | solution.py:801
  46.6 2.3 %collective-permute-done.10 = bf16[2,64,1024]{2,1,0:T(8,128)(2,1)S(1)} collective-permute-done((bf16[2,64,1024]{2,1,0:T(8,128)(2,1)S(1)}, bf16[2,64,1024]{2,1,0:T(8,128)(2,1)S(1)}, u32[]{:S(2)}, u32[]{:S(2)}) %collective-permute-start.10) | collective-permute-done | bytes 262176 | tf_op jit(solution)/shard_map/sum/ppermute | solution.py:618
  48.9 1.6 %collective-permute-start.11 = (bf16[64,1024]{1,0:T(8,128)(2,1)S(1)}, bf16[64,1024]{1,0:T(8,128)(2,1)S(1)}, u32[]{:S(2)}, u32[]{:S(2)}) collective-permute-start(bf16[64,1024]{1,0:T(8,128)(2,1)S(1)} %fusion.9), channel_id=1, source_target_pairs={{0,2},{1,3},{2,0},{3,1},{4,6},{5,7},{6,4},{7,5},{8,10},{9,11},{10,... | collective-permute-start | bytes 393224 | tf_op jit(solution)/shard_map/sum/ppermute | solution.py:618
  50.5 1.5 %collective-permute-start.13 = (bf16[64,1024]{1,0:T(8,128)(2,1)S(1)}, bf16[64,1024]{1,0:T(8,128)(2,1)S(1)}, u32[]{:S(2)}, u32[]{:S(2)}) collective-permute-start(bf16[64,1024]{1,0:T(8,128)(2,1)S(1)} %fusion.6), channel_id=1, source_target_pairs={{0,1},{1,0},{2,3},{3,2},{4,5},{5,4},{6,7},{7,6},{8,9},{9,8},{10,11... | collective-permute-start | bytes 393224 | tf_op jit(solution)/shard_map/sum/ppermute | solution.py:618
  52.1 2.4 %collective-permute-done.14 = bf16[2,64,1024]{2,1,0:T(8,128)(2,1)S(1)} collective-permute-done((bf16[2,64,1024]{2,1,0:T(8,128)(2,1)S(1)}, bf16[2,64,1024]{2,1,0:T(8,128)(2,1)S(1)}, u32[]{:S(2)}, u32[]{:S(2)}) %collective-permute-start.14) | collective-permute-done | bytes 262176 | tf_op jit(solution)/shard_map/sum/ppermute | solution.py:618
  54.5 1.6 %collective-permute-start.15 = (bf16[64,1024]{1,0:T(8,128)(2,1)S(1)}, bf16[64,1024]{1,0:T(8,128)(2,1)S(1)}, u32[]{:S(2)}, u32[]{:S(2)}) collective-permute-start(bf16[64,1024]{1,0:T(8,128)(2,1)S(1)} %fusion.3), channel_id=1, source_target_pairs={{0,2},{1,3},{2,0},{3,1},{4,6},{5,7},{6,4},{7,5},{8,10},{9,11},{10,... | collective-permute-start | bytes 393224 | tf_op jit(solution)/shard_map/sum/ppermute | solution.py:618
  56.2 1.5 %collective-permute-start.17 = (bf16[64,1024]{1,0:T(8,128)(2,1)S(1)}, bf16[64,1024]{1,0:T(8,128)(2,1)S(1)}, u32[]{:S(2)}, u32[]{:S(2)}) collective-permute-start(bf16[64,1024]{1,0:T(8,128)(2,1)S(1)} %fusion), channel_id=1, source_target_pairs={{0,1},{1,0},{2,3},{3,2},{4,5},{5,4},{6,7},{7,6},{8,9},{9,8},{10,11... | collective-permute-start | bytes 393224 | tf_op jit(solution)/shard_map/sum/ppermute | solution.py:618
  57.7 1.1 %collective-permute-done.11 = bf16[64,1024]{1,0:T(8,128)(2,1)S(1)} collective-permute-done((bf16[64,1024]{1,0:T(8,128)(2,1)S(1)}, bf16[64,1024]{1,0:T(8,128)(2,1)S(1)}, u32[]{:S(2)}, u32[]{:S(2)}) %collective-permute-start.11) | collective-permute-done | bytes 131104 | tf_op jit(solution)/shard_map/sum/ppermute | solution.py:618
  58.9 1.6 %collective-permute-done.15 = bf16[64,1024]{1,0:T(8,128)(2,1)S(1)} collective-permute-done((bf16[64,1024]{1,0:T(8,128)(2,1)S(1)}, bf16[64,1024]{1,0:T(8,128)(2,1)S(1)}, u32[]{:S(2)}, u32[]{:S(2)}) %collective-permute-start.15) | collective-permute-done | bytes 131104 | tf_op jit(solution)/shard_map/sum/ppermute | solution.py:618
  61.2 0.8 %pad_maximum_fusion = bf16[64,4096]{1,0:T(8,128)(2,1)} fusion(bf16[64,1024]{1,0:T(8,128)(2,1)S(1)} %fusion.2, bf16[64,1024]{1,0:T(8,128)(2,1)S(1)} %fusion.5, bf16[64,1024]{1,0:T(8,128)(2,1)S(1)} %fusion.8, bf16[64,1024]{1,0:T(8,128)(2,1)S(1)} %fusion.11), kind=kLoop, calls=%fused_computation | loop fusion | flops 2097152 | bytes 1048576 | tf_op jit(solution)/shard_map/sum/concatenate | solution.py:831
  (44 shorter events, 9.0 us)
Async XLA Ops:
  0.6 0.7 %copy-start.8 = (s32[16]{0:T(128)S(1)}, s32[16]{0:T(128)}, u32[]{:S(2)}) copy-start(s32[16]{0:T(128)} %prefix.1) | copy-start | bytes 196
  1.3 35.4 %copy-start.6 = (f32[1024]{0:T(1024)S(1)}, f32[1024]{0:T(1024)}, u32[]{:S(2)}) copy-start(f32[1024]{0:T(1024)} %param.29) | copy-start | bytes 12292
  3.8 1.6 %collective-permute-start.5 = (bf16[2,528,128]{2,1,0:T(8,128)(2,1)S(1)}, bf16[2,528,128]{2,1,0:T(8,128)(2,1)S(1)}, u32[]{:S(2)}, u32[]{:S(2)}) collective-permute-start(bf16[2,528,128]{2,1,0:T(8,128)(2,1)S(1)} %get-tuple-element.69), channel_id=1, source_target_pairs={{0,4},{4,0},{8,12},{12,8},{16,20},{20,16},{24,28},{28,24},{1,5},{5... | collective-permute-start | bytes 811016 | tf_op jit(solution)/shard_map/ppermute | solution.py:614
  6.2 27.9 %collective-permute-start.6 = (bf16[3,528,128]{2,1,0:T(8,128)(2,1)S(1)}, bf16[3,528,128]{2,1,0:T(8,128)(2,1)S(1)}, u32[]{:S(2)}, u32[]{:S(2)}) collective-permute-start(bf16[3,528,128]{2,1,0:T(8,128)(2,1)S(1)} %get-tuple-element.70._), channel_id=1, source_target_pairs={{0,8},{4,12},{8,0},{12,4},{16,24},{20,28},{24,16},{28,20},{1,9},{5... | collective-permute-start | bytes 1216520 | tf_op jit(solution)/shard_map/ppermute | solution.py:614
  6.9 20.3 %collective-permute-start.7 = (bf16[2,528,128]{2,1,0:T(8,128)(2,1)S(1)}, bf16[2,528,128]{2,1,0:T(8,128)(2,1)S(1)}, u32[]{:S(2)}, u32[]{:S(2)}) collective-permute-start(bf16[2,528,128]{2,1,0:T(8,128)(2,1)S(1)} %get-tuple-element.76), channel_id=1, source_target_pairs={{0,16},{4,20},{8,24},{12,28},{16,0},{20,4},{24,8},{28,12},{1,17},{... | collective-permute-start | bytes 811016 | tf_op jit(solution)/shard_map/ppermute | solution.py:614
  10.0 24.1 %collective-permute-start.8 = (bf16[2,528,128]{2,1,0:T(8,128)(2,1)S(1)}, bf16[2,528,128]{2,1,0:T(8,128)(2,1)S(1)}, u32[]{:S(2)}, u32[]{:S(2)}) collective-permute-start(bf16[2,528,128]{2,1,0:T(8,128)(2,1)S(1)} %get-tuple-element.77), channel_id=1, source_target_pairs={{0,24},{4,28},{8,16},{12,20},{16,8},{20,12},{24,0},{28,4},{1,25},{... | collective-permute-start | bytes 811016 | tf_op jit(solution)/shard_map/ppermute | solution.py:614
  10.5 1.0 %copy-start = (bf16[256,1024]{1,0:T(8,128)(2,1)S(1)}, bf16[256,1024]{1,0:T(8,128)(2,1)}, u32[]{:S(2)}) copy-start(bf16[256,1024]{1,0:T(8,128)(2,1)} %x_in.1) | copy-start | bytes 1572868
  11.5 1.0 %copy-start.1 = (bf16[256,1024]{1,0:T(8,128)(2,1)S(1)}, bf16[256,1024]{1,0:T(8,128)(2,1)}, u32[]{:S(2)}) copy-start(bf16[256,1024]{1,0:T(8,128)(2,1)} %z_in.1) | copy-start | bytes 1572868
  12.5 1.0 %copy-start.2 = (bf16[256,1024]{1,0:T(8,128)(2,1)S(1)}, bf16[256,1024]{1,0:T(8,128)(2,1)}, u32[]{:S(2)}) copy-start(bf16[256,1024]{1,0:T(8,128)(2,1)} %bc_in.1) | copy-start | bytes 1572868
  13.6 0.8 %copy-start.3 = (f32[256,32]{0,1:T(8,128)S(1)}, f32[256,32]{0,1:T(8,128)}, u32[]{:S(2)}) copy-start(f32[256,32]{0,1:T(8,128)} %param.23) | copy-start | bytes 98308
  14.3 0.7 %copy-start.4 = (f32[4,1024]{1,0:T(4,128)S(1)}, f32[4,1024]{1,0:T(4,128)}, u32[]{:S(2)}) copy-start(f32[4,1024]{1,0:T(4,128)} %conv_x.1) | copy-start | bytes 49156
  15.1 0.7 %copy-start.5 = (f32[4,1024]{1,0:T(4,128)S(1)}, f32[4,1024]{1,0:T(4,128)}, u32[]{:S(2)}) copy-start(f32[4,1024]{1,0:T(4,128)} %conv_bc.1) | copy-start | bytes 49156
  15.8 0.7 %copy-start.7 = (s32[2]{0:T(128)S(1)}, s32[2]{0:T(128)}, u32[]{:S(2)}) copy-start(s32[2]{0:T(128)} %refs_0_.1) | copy-start | bytes 28
  16.4 0.7 %copy-start.9 = (f32[32]{0:T(128)S(1)}, f32[32]{0:T(128)}, u32[]{:S(2)}) copy-start(f32[32]{0:T(128)} %param.24) | copy-start | bytes 388
  17.1 0.7 %copy-start.10 = (f32[32]{0:T(128)S(1)}, f32[32]{0:T(128)}, u32[]{:S(2)}) copy-start(f32[32]{0:T(128)} %param.25) | copy-start | bytes 388
  35.1 1.6 %collective-permute-start.9 = (bf16[2,528,128]{2,1,0:T(8,128)(2,1)S(1)}, bf16[2,528,128]{2,1,0:T(8,128)(2,1)S(1)}, u32[]{:S(2)}, u32[]{:S(2)}) collective-permute-start(bf16[2,528,128]{2,1,0:T(8,128)(2,1)S(1)} %get-tuple-element.83), channel_id=1, source_target_pairs={{0,4},{4,0},{8,12},{12,8},{16,20},{20,16},{24,28},{28,24},{1,5},{5... | collective-permute-start | bytes 811016 | tf_op jit(solution)/shard_map/ppermute | solution.py:614
  39.6 9.2 %collective-permute-start.10 = (bf16[2,64,1024]{2,1,0:T(8,128)(2,1)S(1)}, bf16[2,64,1024]{2,1,0:T(8,128)(2,1)S(1)}, u32[]{:S(2)}, u32[]{:S(2)}) collective-permute-start(bf16[2,64,1024]{2,1,0:T(8,128)(2,1)S(1)} %get-tuple-element.86), channel_id=1, source_target_pairs={{0,1},{1,0},{2,3},{3,2},{4,5},{5,4},{6,7},{7,6},{8,9},{9,8},{10,11... | collective-permute-start | bytes 786440 | tf_op jit(solution)/shard_map/sum/ppermute | solution.py:618
  41.2 9.3 %collective-permute-start.12 = (bf16[2,64,1024]{2,1,0:T(8,128)(2,1)S(1)}, bf16[2,64,1024]{2,1,0:T(8,128)(2,1)S(1)}, u32[]{:S(2)}, u32[]{:S(2)}) collective-permute-start(bf16[2,64,1024]{2,1,0:T(8,128)(2,1)S(1)} %get-tuple-element.89), channel_id=1, source_target_pairs={{0,2},{1,3},{2,0},{3,1},{4,6},{5,7},{6,4},{7,5},{8,10},{9,11},{10,... | collective-permute-start | bytes 786440 | tf_op jit(solution)/shard_map/sum/ppermute | solution.py:618
  44.0 10.5 %collective-permute-start.14 = (bf16[2,64,1024]{2,1,0:T(8,128)(2,1)S(1)}, bf16[2,64,1024]{2,1,0:T(8,128)(2,1)S(1)}, u32[]{:S(2)}, u32[]{:S(2)}) collective-permute-start(bf16[2,64,1024]{2,1,0:T(8,128)(2,1)S(1)} %get-tuple-element.93), channel_id=1, source_target_pairs={{0,1},{1,0},{2,3},{3,2},{4,5},{5,4},{6,7},{7,6},{8,9},{9,8},{10,11... | collective-permute-start | bytes 786440 | tf_op jit(solution)/shard_map/sum/ppermute | solution.py:618
  44.6 11.5 %collective-permute-start.16 = (bf16[2,64,1024]{2,1,0:T(8,128)(2,1)S(1)}, bf16[2,64,1024]{2,1,0:T(8,128)(2,1)S(1)}, u32[]{:S(2)}, u32[]{:S(2)}) collective-permute-start(bf16[2,64,1024]{2,1,0:T(8,128)(2,1)S(1)} %get-tuple-element.96), channel_id=1, source_target_pairs={{0,2},{1,3},{2,0},{3,1},{4,6},{5,7},{6,4},{7,5},{8,10},{9,11},{10,... | collective-permute-start | bytes 786440 | tf_op jit(solution)/shard_map/sum/ppermute | solution.py:618
  48.9 9.9 %collective-permute-start.11 = (bf16[64,1024]{1,0:T(8,128)(2,1)S(1)}, bf16[64,1024]{1,0:T(8,128)(2,1)S(1)}, u32[]{:S(2)}, u32[]{:S(2)}) collective-permute-start(bf16[64,1024]{1,0:T(8,128)(2,1)S(1)} %fusion.9), channel_id=1, source_target_pairs={{0,2},{1,3},{2,0},{3,1},{4,6},{5,7},{6,4},{7,5},{8,10},{9,11},{10,... | collective-permute-start | bytes 393224 | tf_op jit(solution)/shard_map/sum/ppermute | solution.py:618
  50.5 8.3 %collective-permute-start.13 = (bf16[64,1024]{1,0:T(8,128)(2,1)S(1)}, bf16[64,1024]{1,0:T(8,128)(2,1)S(1)}, u32[]{:S(2)}, u32[]{:S(2)}) collective-permute-start(bf16[64,1024]{1,0:T(8,128)(2,1)S(1)} %fusion.6), channel_id=1, source_target_pairs={{0,1},{1,0},{2,3},{3,2},{4,5},{5,4},{6,7},{7,6},{8,9},{9,8},{10,11... | collective-permute-start | bytes 393224 | tf_op jit(solution)/shard_map/sum/ppermute | solution.py:618
  54.5 6.0 %collective-permute-start.15 = (bf16[64,1024]{1,0:T(8,128)(2,1)S(1)}, bf16[64,1024]{1,0:T(8,128)(2,1)S(1)}, u32[]{:S(2)}, u32[]{:S(2)}) collective-permute-start(bf16[64,1024]{1,0:T(8,128)(2,1)S(1)} %fusion.3), channel_id=1, source_target_pairs={{0,2},{1,3},{2,0},{3,1},{4,6},{5,7},{6,4},{7,5},{8,10},{9,11},{10,... | collective-permute-start | bytes 393224 | tf_op jit(solution)/shard_map/sum/ppermute | solution.py:618
  56.2 5.0 %collective-permute-start.17 = (bf16[64,1024]{1,0:T(8,128)(2,1)S(1)}, bf16[64,1024]{1,0:T(8,128)(2,1)S(1)}, u32[]{:S(2)}, u32[]{:S(2)}) collective-permute-start(bf16[64,1024]{1,0:T(8,128)(2,1)S(1)} %fusion), channel_id=1, source_target_pairs={{0,1},{1,0},{2,3},{3,2},{4,5},{5,4},{6,7},{7,6},{8,9},{9,8},{10,11... | collective-permute-start | bytes 393224 | tf_op jit(solution)/shard_map/sum/ppermute | solution.py:618
  (1 other events, 0.7 us)
where the time goes:
time: 62.6 us; the launch traced here: 62.1 us
  Pallas kernels  18.8 us (30%)
  waiting for transfers between devices  17.9 us (29%)
  starting transfers between devices  14.2 us (23%)
  local copies, waits for them, and re-layouts  8.59 us (14%)
  between operations  1.43 us (2%)
  other arithmetic  1.18 us (2%)
    ppermute x8, starting transfers between devices, over_tensor(): return lax.ppermute(value, 'tensor', [(t, t ^ bits) for t in range(4)])  10.4 us
    ppermute x5, waiting for transfers between devices, over_replica(): return lax.ppermute(value, 'replica', pairs)  9.92 us
    pallas_call x1, Pallas kernels, local_square(): pl.pallas_call(scan_kernel, out_shape=(sds((tokens, ROWS), f32), sds((tok...  8.83 us
    unnamed x24, local copies, waits for them, and re-layouts  8.59 us
    ppermute x8, waiting for transfers between devices, over_tensor(): return lax.ppermute(value, 'tensor', [(t, t ^ bits) for t in range(4)])  8 us
    ppermute x5, starting transfers between devices, over_replica(): return lax.ppermute(value, 'replica', pairs)  3.76 us
    pallas_call x1, Pallas kernels, local_square(): call(out_shape=[sds((tokens, ROWS), bf16), sds((SLOTS, 8, ROWS), f32), sd...  2.95 us
    pallas_call x1, Pallas kernels, local_square(): pl.pallas_call(pack_kernel, out_shape=(sds((SLOTS, ITEM_ROWS, LANES), bf1...  2.53 us
  transfers between devices with their start and end apart: 13, of which 8 were waited for; matrix products, arithmetic and copies ran while one was open for 0% of the time, Pallas kernels for 19%

commit v1 on v0

--- a/solution.py
+++ b/solution.py
@@ -195,14 +195,11 @@
 
 
 def pack_kernel(
-    prefix,
     states,
     tail_x,
     tail_bc,
     send,
     keep,
-    plan,
-    variant,
     blocks,
     rows_x,
     rows_bc,
@@ -219,7 +216,6 @@
     ]
     for copy in copies:
         copy.start()
-    make_plan(prefix, plan, variant)
     for copy in copies:
         copy.wait()
     scratch[...] = jnp.zeros_like(scratch)
@@ -239,7 +235,7 @@
             out[block, HALF:, :] = scratch[tail_half(half), :].astype(bf16)
 
 
-def make_plan(prefix, plan, variant):
+def plan_kernel(prefix, plan, variant):
     chip, core = chip_and_core()
     need = [jnp.int32(0)] * CHIPS
     for entry in range(PLACE_PLAN):
@@ -289,7 +285,7 @@
         out[at] = recv[slot]
 
 
-def select_kernel(first, counts, plan, keep, recv, *outs):
+def select_kernel(first, counts, plan, _, keep, recv, *outs):
     _, core = chip_and_core()
     outs = iter(outs)
     for d in range(1, CHIPS):
@@ -308,30 +304,29 @@
             out[:n] = next(came)[...]
 
 
-def place_kernel(plan, _, keep, recv, *refs):
-    came, (mine, other) = refs[: 2 * (CHIPS - 1)], refs[-2:]
+def place_kernel(owner, plan, _, keep, recv, *refs):
+    came, out = refs[: 2 * (CHIPS - 1)], refs[-1]
     _, core = chip_and_core()
-    for o, out in enumerate((other, mine)):
-        for slot in range(SLOTS):
-            code = plan[PLACE_PLAN + (1 - o) * SLOTS + slot]
-            d = code // ITEMS
-            which = lax.rem(code, ITEMS)
-
-            @pl.when(d == 0)
+    for slot in range(SLOTS):
+        code = plan[PLACE_PLAN + owner * SLOTS + slot]
+        d = code // ITEMS
+        which = lax.rem(code, ITEMS)
+
+        @pl.when(d == 0)
+        def _():
+            copy_item(out, slot, keep, recv, which, core)
+
+        for e in range(1, CHIPS):
+            few = BASE[e - 1]
+            base, extra = came[e - 1], came[e + 2]
+
+            @pl.when((d == e) & (which < few))
             def _():
-                copy_item(out, slot, keep, recv, which, core)
-
-            for e in range(1, CHIPS):
-                few = BASE[e - 1]
-                base, extra = came[e - 1], came[e + 2]
-
-                @pl.when((d == e) & (which < few))
-                def _():
-                    out[slot] = base[jnp.minimum(which, few - 1)]
-
-                @pl.when((d == e) & (which >= few))
-                def _():
-                    out[slot] = extra[jnp.maximum(which - few, 0)]
+                out[slot] = base[jnp.minimum(which, few - 1)]
+
+            @pl.when((d == e) & (which >= few))
+            def _():
+                out[slot] = extra[jnp.maximum(which - few, 0)]
 
 
 def scan_kernel(
@@ -482,10 +477,9 @@
     return wide.reshape(heads * HEAD_DIM, LANES)
 
 
-def first_tokens(early, tails):
+def first_tokens(early, tail):
     row = lax.broadcasted_iota(jnp.int32, (8, WIDE), 0)
     taps = early[1]
-    tail = tails[...]
     total = early[0]
     for t in range(EARLY):
         add = sum(taps[k : k + 1] * tail[t + k : t + k + 1] for k in range(EARLY - t))
@@ -523,14 +517,14 @@
     tail_rows[...] = jnp.zeros_like(tail_rows)
     for r in range(SLOTS):
         rows = slice(r * span, (r + 1) * span)
-        start[half_at(core), :] = mine[r, :HALF]
-        start[half_at(1 - core), :] = other[r, :HALF]
-        tails[tail_half(core), :] = mine[r, HALF:].astype(f32)
-        tails[tail_half(1 - core), :] = other[r, HALF:].astype(f32)
+        start[r, half_at(core), :] = mine[r, :HALF]
+        start[r, half_at(1 - core), :] = other[r, :HALF]
+        tails[r, tail_half(core), :] = mine[r, HALF:].astype(f32)
+        tails[r, tail_half(1 - core), :] = other[r, HALF:].astype(f32)
         for s in range(COLUMN_BLOCKS + 2):
-            tail_rows[:EARLY, s * LANES : (s + 1) * LANES] = tails[3 * s : 3 * s + 3, :]
-
-        x_8, b_8, c_8 = first_tokens(early[r], tail_rows)
+            tail_rows[r, :EARLY, s * LANES : (s + 1) * LANES] = tails[r, 3 * s : 3 * s + 3, :]
+
+        x_8, b_8, c_8 = first_tokens(early[r], tail_rows[r])
         steps, cum, gate_8 = early[r, 2, :, :ROWS], early[r, 3, :, :ROWS], early[r, 4, :, :ROWS]
         skip = early[r, 5, 0:1, :ROWS]
         moved = steps * x_8
@@ -538,11 +532,11 @@
         kept = jnp.where(row < EARLY, jnp.exp2(jnp.minimum(last - cum, 0.0)) * moved, 0.0)
         x_first[r] = kept
         b_first[r] = b_8
-        after = by_head(start[...], e_scale[r]) + lax.dot_general(
+        after = by_head(start[r], e_scale[r]) + lax.dot_general(
             kept, b_8, over_first, preferred_element_type=f32
         )
         y_8 = skip * x_8 + jnp.exp2(cum) * lax.dot_general(
-            c_8.astype(bf16), start[...], over_last, preferred_element_type=f32
+            c_8.astype(bf16), start[r], over_last, preferred_element_type=f32
         )
         scores = lax.dot_general(c_8, b_8, over_last, preferred_element_type=f32)
         for j in range(EARLY):
@@ -618,15 +612,15 @@
     return lax.ppermute(value, "tensor", [(t, t ^ bits) for t in range(4)])
 
 
-def select(first, counts, plan, keep, recv):
+def select(first, counts, plan, after, keep, recv):
     with jax.named_scope("select"):
         return pl.pallas_call(
             partial(select_kernel, first, counts),
             out_shape=[sds((n, ITEM_ROWS, LANES), bf16) for n in counts if n],
-            in_specs=[SMEM, VMEM, VMEM],
+            in_specs=[SMEM, ANYWHERE, VMEM, VMEM],
             out_specs=[VMEM for n in counts if n],
             compiler_params=params(),
-        )(plan, keep, recv)
+        )(plan, after, keep, recv)
 
 
 def exchange(counts, sends):
@@ -635,7 +629,7 @@
 
 
 def migrate_more(counts, plan, keep, recv):
-    came = exchange(counts, select(BASE, counts, plan, keep, recv)) if any(counts) else []
+    came = exchange(counts, select(BASE, counts, plan, keep, keep, recv)) if any(counts) else []
     return pl.pallas_call(
         partial(spread_kernel, counts),
         out_shape=tuple(sds((n, ITEM_ROWS, LANES), bf16) for n in EXTRAS[-1]),
@@ -669,12 +663,11 @@
     span = tokens // SLOTS
 
     with jax.named_scope("pack"):
-        send, keep, plan, variant = pl.pallas_call(
+        send, keep = pl.pallas_call(
             pack_kernel,
-            out_shape=(sds((SLOTS, ITEM_ROWS, LANES), bf16),) * 2
-            + (sds((PLACE_PLAN + ITEMS,), jnp.int32), sds((1,), jnp.int32)),
-            in_specs=[SMEM, HBM, HBM, HBM],
-            out_specs=(VMEM, VMEM, SMEM, SMEM),
+            out_shape=(sds((SLOTS, ITEM_ROWS, LANES), bf16),) * 2,
+            in_specs=[HBM] * 3,
+            out_specs=(VMEM, VMEM),
             scratch_shapes=[
                 pltpu.VMEM((2, SLOTS, HALF, LANES), f32),
                 pltpu.VMEM((CONV - 1, SLOTS) + cached_tail_x.shape[2:], f32),
@@ -684,12 +677,20 @@
             ],
             compiler_params=params(),
         )(
-            prefix_block,
             in_hbm(cached_states.reshape(SLOTS, ROWS, LANES)),
             in_hbm(jnp.transpose(cached_tail_x, (1, 0, 2))),
             in_hbm(jnp.transpose(cached_tail_bc, (1, 0, 2))),
         )
     recv = over_replica(send, 1)
+    with jax.named_scope("plan"):
+        plan, variant = pl.pallas_call(
+            plan_kernel,
+            out_shape=(sds((PLACE_PLAN + ITEMS,), jnp.int32), sds((1,), jnp.int32)),
+            in_specs=[SMEM],
+            out_specs=(SMEM, SMEM),
+            compiler_params=params(),
+        )(in_hbm(prefix_block))
+
     more = lax.switch(
         variant.reshape(()),
         [partial(migrate_more, counts) for counts in EXTRAS],
@@ -697,7 +698,7 @@
         keep,
         recv,
     )
-    sends = select((0,) * (CHIPS - 1), BASE, plan, keep, recv)
+    sends = select((0,) * (CHIPS - 1), BASE, plan, more[0], keep, recv)
     came = exchange(BASE, sends)
 
     with jax.named_scope("scan"):
@@ -734,15 +735,19 @@
             in_hbm(out_weight),
         )
 
-    with jax.named_scope("place"):
-        mine, theirs = pl.pallas_call(
-            place_kernel,
-            out_shape=(sds((SLOTS, ITEM_ROWS, LANES), bf16),) * 2,
-            in_specs=[SMEM, ANYWHERE] + [VMEM] * 8,
-            out_specs=(VMEM, VMEM),
-            compiler_params=params(),
-        )(plan, c_mat, keep, recv, *came, *more)
+    def place(owner, after):
+        with jax.named_scope("place"):
+            return pl.pallas_call(
+                partial(place_kernel, owner),
+                out_shape=sds((SLOTS, ITEM_ROWS, LANES), bf16),
+                in_specs=[SMEM, ANYWHERE] + [VMEM] * 8,
+                out_specs=VMEM,
+                compiler_params=params(),
+            )(plan, after, keep, recv, *came, *more)
+
+    theirs = place(1, c_mat)
     other = over_replica(theirs, 1)
+    mine = place(0, theirs)
 
     quarter = tokens // 4
     pieces = []
@@ -769,9 +774,9 @@
                     in_specs=[SMEM] + [VMEM] * 9,
                     out_specs=[VMEM] * 9,
                     scratch_shapes=[
-                        pltpu.VMEM((ROWS, LANES), bf16),
-                        pltpu.VMEM((TAIL, LANES), f32),
-                        pltpu.VMEM((8, WIDE), f32),
+                        pltpu.VMEM((SLOTS, ROWS, LANES), bf16),
+                        pltpu.VMEM((SLOTS, TAIL, LANES), f32),
+                        pltpu.VMEM((SLOTS, 8, WIDE), f32),
                     ],
                 )(
                     lengths,

time: 62.6 us -> 60.7 us (0.970)
  waiting for transfers between devices: 17.9 us -> 15.8 us
  Pallas kernels: 18.8 us -> 19.6 us
  local copies, waits for them, and re-layouts: 8.59 us -> 7.94 us
    ppermute x5, waiting for transfers between devices: 9.92 us -> 7.89 us  [over_replica(): return lax.ppermute(value, 'replica', pairs)]
    pallas_call x1 -> x3, Pallas kernels: 0.97 us -> 2.95 us  [the longest x2 1.51 us: place(): pl.pallas_call(partial(place_kernel, owner), out_shape=sds((SLOTS, ITEM_R...]
    pallas_call x1, Pallas kernels: 2.53 us -> 1.36 us  [local_square(): pl.pallas_call(pack_kernel, out_shape=(sds((SLOTS, ITEM_ROWS, LANES), bf1...]
    unnamed x24 -> x22, local copies, waits for them, and re-layouts: 8.59 us -> 7.94 us
  transfers between devices with their start and end apart: 13 -> 13, of which waited for: 8 -> 7; matrix products, arithmetic and copies ran while one was open for 0% -> 1% of each run, Pallas kernels for 19% -> 23%
where the time goes in v1:
time: 60.7 us; the launch traced here: 60.2 us
  Pallas kernels  19.6 us (32%)
  waiting for transfers between devices  15.8 us (26%)
  starting transfers between devices  14.2 us (23%)
  local copies, waits for them, and re-layouts  7.94 us (13%)
  between operations  1.46 us (2%)
  other arithmetic  1.2 us (2%)
    ppermute x8, starting transfers between devices, over_tensor(): return lax.ppermute(value, 'tensor', [(t, t ^ bits) for t in range(4)])  10.5 us
    pallas_call x1, Pallas kernels, local_square(): pl.pallas_call(scan_kernel, out_shape=(sds((tokens, ROWS), f32), sds((tok...  8.83 us
    unnamed x22, local copies, waits for them, and re-layouts  7.94 us
    ppermute x8, waiting for transfers between devices, over_tensor(): return lax.ppermute(value, 'tensor', [(t, t ^ bits) for t in range(4)])  7.91 us
    ppermute x5, waiting for transfers between devices, over_replica(): return lax.ppermute(value, 'replica', pairs)  7.89 us
    ppermute x5, starting transfers between devices, over_replica(): return lax.ppermute(value, 'replica', pairs)  3.69 us
    pallas_call x1, Pallas kernels, local_square(): call(out_shape=[sds((tokens, ROWS), bf16), sds((SLOTS, 8, ROWS), f32), sd...  2.95 us
    pallas_call x2, Pallas kernels, place(): pl.pallas_call(partial(place_kernel, owner), out_shape=sds((SLOTS, ITEM_R...  1.51 us
  transfers between devices with their start and end apart: 13, of which 7 were waited for; matrix products, arithmetic and copies ran while one was open for 1% of the time, Pallas kernels for 23%

profile of v1, /device:TPU:8, one launch (start us, length us, event | category | flops | bytes accessed | tf_op | source)
XLA Modules:
  0.0 60.2 jit_solution(820373331781951678)
XLA Ops:
  0.6 1.4 %pack.1 = (bf16[2,528,128]{2,1,0:T(8,128)(2,1)S(1)}, bf16[2,528,128]{2,1,0:T(8,128)(2,1)S(1)}) custom-call(f32[2,1024,128]{2,1,0:T(8,128)} %bitcast.55, f32[3,2,1024]{2,1,0:T(2,128)} %bitcast.57, f32[3,2,1024]{2,1,0:T(2,128)} %bitcast.58), custom_call_target="tpu_custom_call" | custom-call | tf_op jit(solution)/shard_map/pack/pallas_call | solution.py:666
  2.1 1.4 %plan.1 = (s32[16]{0:T(128)S(1)}, s32[1]{0:T(128)}) custom-call(s32[16]{0:T(128)} %prefix.1), custom_call_target="tpu_custom_call" | custom-call | tf_op jit(solution)/shard_map/plan/pallas_call | solution.py:686
  5.0 3.0 %collective-permute-start.7 = (bf16[2,528,128]{2,1,0:T(8,128)(2,1)S(1)}, bf16[2,528,128]{2,1,0:T(8,128)(2,1)S(1)}, u32[]{:S(2)}, u32[]{:S(2)}) collective-permute-start(bf16[2,528,128]{2,1,0:T(8,128)(2,1)S(1)} %get-tuple-element.76), channel_id=1, source_target_pairs={{0,16},{4,20},{8,24},{12,28},{16,0},{20,4},{24,8},{28,12},{1,17},{... | collective-permute-start | bytes 811016 | tf_op jit(solution)/shard_map/ppermute | solution.py:608
  8.5 1.0 %copy-done = bf16[256,1024]{1,0:T(8,128)(2,1)S(1)} copy-done((bf16[256,1024]{1,0:T(8,128)(2,1)S(1)}, bf16[256,1024]{1,0:T(8,128)(2,1)}, u32[]{:S(2)}) %copy-start) | copy-done | bytes 524312
  9.6 1.0 %copy-done.1 = bf16[256,1024]{1,0:T(8,128)(2,1)S(1)} copy-done((bf16[256,1024]{1,0:T(8,128)(2,1)S(1)}, bf16[256,1024]{1,0:T(8,128)(2,1)}, u32[]{:S(2)}) %copy-start.1) | copy-done | bytes 524312
  10.6 1.0 %copy-done.2 = bf16[256,1024]{1,0:T(8,128)(2,1)S(1)} copy-done((bf16[256,1024]{1,0:T(8,128)(2,1)S(1)}, bf16[256,1024]{1,0:T(8,128)(2,1)}, u32[]{:S(2)}) %copy-start.2) | copy-done | bytes 524312
  11.7 0.8 %copy-done.3 = f32[256,32]{0,1:T(8,128)S(1)} copy-done((f32[256,32]{0,1:T(8,128)S(1)}, f32[256,32]{0,1:T(8,128)}, u32[]{:S(2)}) %copy-start.3) | copy-done | bytes 32792
  16.5 8.8 %scan.1 = (f32[256,1024]{1,0:T(8,128)S(1)}, f32[256,1024]{1,0:T(8,128)S(1)}, bf16[256,128]{1,0:T(8,128)(2,1)S(1)}, f32[2,1024,128]{2,1,0:T(8,128)S(1)}, f32[2,32...) custom-call(bf16[3,528,128]{2,1,0:T(8,128)(2,1)S(1)} %get-tuple-elem, ...), custom_call_target="tpu_custom_call" | custom-call | flops 1073741824 | bytes 8388608 | tf_op jit(solution)/shard_map/scan/pallas_call | solution.py:706
  25.3 7.2 %collective-permute-done.8.refs_2_ = bf16[2,528,128]{2,1,0:T(8,128)(2,1)S(1)} collective-permute-done((bf16[2,528,128]{2,1,0:T(8,128)(2,1)S(1)}, bf16[2,528,128]{2,1,0:T(8,128)(2,1)S(1)}, u32[]{:S(2)}, u32[]{:S(2)}) %collective-permute-start.8) | collective-permute-done | bytes 270368 | tf_op jit(solution)/shard_map/ppermute | solution.py:608
  33.3 0.9 %place.3.refs_6_.mine = bf16[2,528,128]{2,1,0:T(8,128)(2,1)S(1)} custom-call(s32[16]{0:T(128)S(1)} %get-tuple-element.65.plan, bf16[2,528,128]{2,1,0:T(8,128)(2,1)S(1)} %place.2._, bf16[2,528,128]{2,1,0:T(8,128)(2,1)S(1)} %get-tuple-element.67.keep, bf16[2,528,128]{2,1,0:T(8,128)(2,1)S(1)} %collective-permute-done.5.recv, ...), custom_call_target="tpu_custom_call" | custom-call | tf_op jit(solution)/shard_map/place/pallas_call | solution.py:740
  34.8 2.9 %project.2 = (bf16[256,1024]{1,0:T(8,128)(2,1)S(1)}, f32[2,8,1024]{2,1,0:T(8,128)S(1)}, f32[2,8,128]{2,1,0:T(8,128)S(1)}, bf16[2,64,1024]{2,1,0:T(8,128)(2,1)S(1...) custom-call(s32[2]{0:T(128)S(1)} %copy-done.7, ...), custom_call_target="tpu_custom_call" | custom-call | flops 1073741824 | bytes 4194304 | tf_op jit(solution)/shard_map/project/pallas_call | solution.py:767
  37.8 1.6 %collective-permute-start.10 = (bf16[2,64,1024]{2,1,0:T(8,128)(2,1)S(1)}, bf16[2,64,1024]{2,1,0:T(8,128)(2,1)S(1)}, u32[]{:S(2)}, u32[]{:S(2)}) collective-permute-start(bf16[2,64,1024]{2,1,0:T(8,128)(2,1)S(1)} %get-tuple-element.82), channel_id=1, source_target_pairs={{0,1},{1,0},{2,3},{3,2},{4,5},{5,4},{6,7},{7,6},{8,9},{9,8},{10,11... | collective-permute-start | bytes 786440 | tf_op jit(solution)/shard_map/sum/ppermute | solution.py:612
  39.3 1.5 %collective-permute-start.12 = (bf16[2,64,1024]{2,1,0:T(8,128)(2,1)S(1)}, bf16[2,64,1024]{2,1,0:T(8,128)(2,1)S(1)}, u32[]{:S(2)}, u32[]{:S(2)}) collective-permute-start(bf16[2,64,1024]{2,1,0:T(8,128)(2,1)S(1)} %get-tuple-element.85), channel_id=1, source_target_pairs={{0,2},{1,3},{2,0},{3,1},{4,6},{5,7},{6,4},{7,5},{8,10},{9,11},{10,... | collective-permute-start | bytes 786440 | tf_op jit(solution)/shard_map/sum/ppermute | solution.py:612
  40.9 1.3 %project.3 = (bf16[2,64,1024]{2,1,0:T(8,128)(2,1)S(1)}, bf16[64,1024]{1,0:T(8,128)(2,1)S(1)}, bf16[64,1024]{1,0:T(8,128)(2,1)S(1)}, bf16[2,64,1024]{2,1,0:T(8,12...) custom-call(bf16[256,1024]{1,0:T(8,128)(2,1)S(1)} %get-tuple-element.87.refs_0_, ...), custom_call_target="tpu_custom_call" | custom-call | flops 1073741824 | bytes 4194304 | tf_op jit(solution)/shard_map/project/pallas_call | solution.py:794
  43.2 1.5 %final_states.1 = f32[2,1024,128]{2,1,0:T(8,128)} custom-call(bf16[2,528,128]{2,1,0:T(8,128)(2,1)S(1)} %place.3.refs_6_.mine, bf16[2,528,128]{2,1,0:T(8,128)(2,1)S(1)} %collective-permute-done.9.refs_7_.other, f32[2,8,1024]{2,1,0:T(8,128)S(1)} %get-tuple-element.94.x_first, f32[2,8,128]{2,1,0:T(8,128)S(1)} %get-tuple-element.95.b_first, ...), custom_call_target="tpu_custom_call" | custom-call | bytes 4194304 | tf_op jit(solution)/shard_map/final_states/pallas_call | solution.py:806
  44.7 2.3 %collective-permute-done.10 = bf16[2,64,1024]{2,1,0:T(8,128)(2,1)S(1)} collective-permute-done((bf16[2,64,1024]{2,1,0:T(8,128)(2,1)S(1)}, bf16[2,64,1024]{2,1,0:T(8,128)(2,1)S(1)}, u32[]{:S(2)}, u32[]{:S(2)}) %collective-permute-start.10) | collective-permute-done | bytes 262176 | tf_op jit(solution)/shard_map/sum/ppermute | solution.py:612
  47.0 1.6 %collective-permute-start.11 = (bf16[64,1024]{1,0:T(8,128)(2,1)S(1)}, bf16[64,1024]{1,0:T(8,128)(2,1)S(1)}, u32[]{:S(2)}, u32[]{:S(2)}) collective-permute-start(bf16[64,1024]{1,0:T(8,128)(2,1)S(1)} %fusion.9), channel_id=1, source_target_pairs={{0,2},{1,3},{2,0},{3,1},{4,6},{5,7},{6,4},{7,5},{8,10},{9,11},{10,... | collective-permute-start | bytes 393224 | tf_op jit(solution)/shard_map/sum/ppermute | solution.py:612
  48.6 1.6 %collective-permute-start.13 = (bf16[64,1024]{1,0:T(8,128)(2,1)S(1)}, bf16[64,1024]{1,0:T(8,128)(2,1)S(1)}, u32[]{:S(2)}, u32[]{:S(2)}) collective-permute-start(bf16[64,1024]{1,0:T(8,128)(2,1)S(1)} %fusion.6), channel_id=1, source_target_pairs={{0,1},{1,0},{2,3},{3,2},{4,5},{5,4},{6,7},{7,6},{8,9},{9,8},{10,11... | collective-permute-start | bytes 393224 | tf_op jit(solution)/shard_map/sum/ppermute | solution.py:612
  50.2 2.4 %collective-permute-done.14 = bf16[2,64,1024]{2,1,0:T(8,128)(2,1)S(1)} collective-permute-done((bf16[2,64,1024]{2,1,0:T(8,128)(2,1)S(1)}, bf16[2,64,1024]{2,1,0:T(8,128)(2,1)S(1)}, u32[]{:S(2)}, u32[]{:S(2)}) %collective-permute-start.14) | collective-permute-done | bytes 262176 | tf_op jit(solution)/shard_map/sum/ppermute | solution.py:612
  52.6 1.6 %collective-permute-start.15 = (bf16[64,1024]{1,0:T(8,128)(2,1)S(1)}, bf16[64,1024]{1,0:T(8,128)(2,1)S(1)}, u32[]{:S(2)}, u32[]{:S(2)}) collective-permute-start(bf16[64,1024]{1,0:T(8,128)(2,1)S(1)} %fusion.3), channel_id=1, source_target_pairs={{0,2},{1,3},{2,0},{3,1},{4,6},{5,7},{6,4},{7,5},{8,10},{9,11},{10,... | collective-permute-start | bytes 393224 | tf_op jit(solution)/shard_map/sum/ppermute | solution.py:612
  54.3 1.6 %collective-permute-start.17 = (bf16[64,1024]{1,0:T(8,128)(2,1)S(1)}, bf16[64,1024]{1,0:T(8,128)(2,1)S(1)}, u32[]{:S(2)}, u32[]{:S(2)}) collective-permute-start(bf16[64,1024]{1,0:T(8,128)(2,1)S(1)} %fusion), channel_id=1, source_target_pairs={{0,1},{1,0},{2,3},{3,2},{4,5},{5,4},{6,7},{7,6},{8,9},{9,8},{10,11... | collective-permute-start | bytes 393224 | tf_op jit(solution)/shard_map/sum/ppermute | solution.py:612
  55.8 1.1 %collective-permute-done.11 = bf16[64,1024]{1,0:T(8,128)(2,1)S(1)} collective-permute-done((bf16[64,1024]{1,0:T(8,128)(2,1)S(1)}, bf16[64,1024]{1,0:T(8,128)(2,1)S(1)}, u32[]{:S(2)}, u32[]{:S(2)}) %collective-permute-start.11) | collective-permute-done | bytes 131104 | tf_op jit(solution)/shard_map/sum/ppermute | solution.py:612
  57.1 1.5 %collective-permute-done.15 = bf16[64,1024]{1,0:T(8,128)(2,1)S(1)} collective-permute-done((bf16[64,1024]{1,0:T(8,128)(2,1)S(1)}, bf16[64,1024]{1,0:T(8,128)(2,1)S(1)}, u32[]{:S(2)}, u32[]{:S(2)}) %collective-permute-start.15) | collective-permute-done | bytes 131104 | tf_op jit(solution)/shard_map/sum/ppermute | solution.py:612
  59.4 0.8 %pad_maximum_fusion = bf16[64,4096]{1,0:T(8,128)(2,1)} fusion(bf16[64,1024]{1,0:T(8,128)(2,1)S(1)} %fusion.2, bf16[64,1024]{1,0:T(8,128)(2,1)S(1)} %fusion.5, bf16[64,1024]{1,0:T(8,128)(2,1)S(1)} %fusion.8, bf16[64,1024]{1,0:T(8,128)(2,1)S(1)} %fusion.11), kind=kLoop, calls=%fused_computation | loop fusion | flops 2097152 | bytes 1048576 | tf_op jit(solution)/shard_map/sum/concatenate | solution.py:836
  (44 shorter events, 8.9 us)
Async XLA Ops:
  2.0 2.2 %collective-permute-start.5 = (bf16[2,528,128]{2,1,0:T(8,128)(2,1)S(1)}, bf16[2,528,128]{2,1,0:T(8,128)(2,1)S(1)}, u32[]{:S(2)}, u32[]{:S(2)}) collective-permute-start(bf16[2,528,128]{2,1,0:T(8,128)(2,1)S(1)} %get-tuple-element.68), channel_id=1, source_target_pairs={{0,4},{4,0},{8,12},{12,8},{16,20},{20,16},{24,28},{28,24},{1,5},{5... | collective-permute-start | bytes 811016 | tf_op jit(solution)/shard_map/ppermute | solution.py:608
  4.2 30.6 %copy-start.6 = (f32[1024]{0:T(1024)S(1)}, f32[1024]{0:T(1024)}, u32[]{:S(2)}) copy-start(f32[1024]{0:T(1024)} %param.29) | copy-start | bytes 12292
  5.0 27.6 %collective-permute-start.6 = (bf16[3,528,128]{2,1,0:T(8,128)(2,1)S(1)}, bf16[3,528,128]{2,1,0:T(8,128)(2,1)S(1)}, u32[]{:S(2)}, u32[]{:S(2)}) collective-permute-start(bf16[3,528,128]{2,1,0:T(8,128)(2,1)S(1)} %get-tuple-element.70._), channel_id=1, source_target_pairs={{0,8},{4,12},{8,0},{12,4},{16,24},{20,28},{24,16},{28,20},{1,9},{5... | collective-permute-start | bytes 1216520 | tf_op jit(solution)/shard_map/ppermute | solution.py:608
  5.0 20.3 %collective-permute-start.7 = (bf16[2,528,128]{2,1,0:T(8,128)(2,1)S(1)}, bf16[2,528,128]{2,1,0:T(8,128)(2,1)S(1)}, u32[]{:S(2)}, u32[]{:S(2)}) collective-permute-start(bf16[2,528,128]{2,1,0:T(8,128)(2,1)S(1)} %get-tuple-element.76), channel_id=1, source_target_pairs={{0,16},{4,20},{8,24},{12,28},{16,0},{20,4},{24,8},{28,12},{1,17},{... | collective-permute-start | bytes 811016 | tf_op jit(solution)/shard_map/ppermute | solution.py:608
  8.1 24.5 %collective-permute-start.8 = (bf16[2,528,128]{2,1,0:T(8,128)(2,1)S(1)}, bf16[2,528,128]{2,1,0:T(8,128)(2,1)S(1)}, u32[]{:S(2)}, u32[]{:S(2)}) collective-permute-start(bf16[2,528,128]{2,1,0:T(8,128)(2,1)S(1)} %get-tuple-element.77), channel_id=1, source_target_pairs={{0,24},{4,28},{8,16},{12,20},{16,8},{20,12},{24,0},{28,4},{1,25},{... | collective-permute-start | bytes 811016 | tf_op jit(solution)/shard_map/ppermute | solution.py:608
  8.5 1.0 %copy-start = (bf16[256,1024]{1,0:T(8,128)(2,1)S(1)}, bf16[256,1024]{1,0:T(8,128)(2,1)}, u32[]{:S(2)}) copy-start(bf16[256,1024]{1,0:T(8,128)(2,1)} %x_in.1) | copy-start | bytes 1572868
  9.6 1.0 %copy-start.1 = (bf16[256,1024]{1,0:T(8,128)(2,1)S(1)}, bf16[256,1024]{1,0:T(8,128)(2,1)}, u32[]{:S(2)}) copy-start(bf16[256,1024]{1,0:T(8,128)(2,1)} %z_in.1) | copy-start | bytes 1572868
  10.6 1.0 %copy-start.2 = (bf16[256,1024]{1,0:T(8,128)(2,1)S(1)}, bf16[256,1024]{1,0:T(8,128)(2,1)}, u32[]{:S(2)}) copy-start(bf16[256,1024]{1,0:T(8,128)(2,1)} %bc_in.1) | copy-start | bytes 1572868
  11.6 0.8 %copy-start.3 = (f32[256,32]{0,1:T(8,128)S(1)}, f32[256,32]{0,1:T(8,128)}, u32[]{:S(2)}) copy-start(f32[256,32]{0,1:T(8,128)} %param.23) | copy-start | bytes 98308
  12.4 0.7 %copy-start.4 = (f32[4,1024]{1,0:T(4,128)S(1)}, f32[4,1024]{1,0:T(4,128)}, u32[]{:S(2)}) copy-start(f32[4,1024]{1,0:T(4,128)} %conv_x.1) | copy-start | bytes 49156
  13.1 0.7 %copy-start.5 = (f32[4,1024]{1,0:T(4,128)S(1)}, f32[4,1024]{1,0:T(4,128)}, u32[]{:S(2)}) copy-start(f32[4,1024]{1,0:T(4,128)} %conv_bc.1) | copy-start | bytes 49156
  13.8 0.7 %copy-start.7 = (s32[2]{0:T(128)S(1)}, s32[2]{0:T(128)}, u32[]{:S(2)}) copy-start(s32[2]{0:T(128)} %refs_0_.1) | copy-start | bytes 28
  14.5 0.7 %copy-start.8 = (f32[32]{0:T(128)S(1)}, f32[32]{0:T(128)}, u32[]{:S(2)}) copy-start(f32[32]{0:T(128)} %param.24) | copy-start | bytes 388
  15.2 0.7 %copy-start.9 = (f32[32]{0:T(128)S(1)}, f32[32]{0:T(128)}, u32[]{:S(2)}) copy-start(f32[32]{0:T(128)} %param.25) | copy-start | bytes 388
  15.8 0.7 %copy-start.10 = (f32[32]{0:T(128)S(1)}, f32[32]{0:T(128)}, u32[]{:S(2)}) copy-start(f32[32]{0:T(128)} %param.26) | copy-start | bytes 388
  33.2 1.6 %collective-permute-start.9 = (bf16[2,528,128]{2,1,0:T(8,128)(2,1)S(1)}, bf16[2,528,128]{2,1,0:T(8,128)(2,1)S(1)}, u32[]{:S(2)}, u32[]{:S(2)}) collective-permute-start(bf16[2,528,128]{2,1,0:T(8,128)(2,1)S(1)} %place.2._), channel_id=1, source_target_pairs={{0,4},{4,0},{8,12},{12,8},{16,20},{20,16},{24,28},{28,24},{1,5},{5... | collective-permute-start | bytes 811016 | tf_op jit(solution)/shard_map/ppermute | solution.py:608
  37.8 9.2 %collective-permute-start.10 = (bf16[2,64,1024]{2,1,0:T(8,128)(2,1)S(1)}, bf16[2,64,1024]{2,1,0:T(8,128)(2,1)S(1)}, u32[]{:S(2)}, u32[]{:S(2)}) collective-permute-start(bf16[2,64,1024]{2,1,0:T(8,128)(2,1)S(1)} %get-tuple-element.82), channel_id=1, source_target_pairs={{0,1},{1,0},{2,3},{3,2},{4,5},{5,4},{6,7},{7,6},{8,9},{9,8},{10,11... | collective-permute-start | bytes 786440 | tf_op jit(solution)/shard_map/sum/ppermute | solution.py:612
  39.3 9.3 %collective-permute-start.12 = (bf16[2,64,1024]{2,1,0:T(8,128)(2,1)S(1)}, bf16[2,64,1024]{2,1,0:T(8,128)(2,1)S(1)}, u32[]{:S(2)}, u32[]{:S(2)}) collective-permute-start(bf16[2,64,1024]{2,1,0:T(8,128)(2,1)S(1)} %get-tuple-element.85), channel_id=1, source_target_pairs={{0,2},{1,3},{2,0},{3,1},{4,6},{5,7},{6,4},{7,5},{8,10},{9,11},{10,... | collective-permute-start | bytes 786440 | tf_op jit(solution)/shard_map/sum/ppermute | solution.py:612
  42.1 10.5 %collective-permute-start.14 = (bf16[2,64,1024]{2,1,0:T(8,128)(2,1)S(1)}, bf16[2,64,1024]{2,1,0:T(8,128)(2,1)S(1)}, u32[]{:S(2)}, u32[]{:S(2)}) collective-permute-start(bf16[2,64,1024]{2,1,0:T(8,128)(2,1)S(1)} %get-tuple-element.89), channel_id=1, source_target_pairs={{0,1},{1,0},{2,3},{3,2},{4,5},{5,4},{6,7},{7,6},{8,9},{9,8},{10,11... | collective-permute-start | bytes 786440 | tf_op jit(solution)/shard_map/sum/ppermute | solution.py:612
  42.7 11.5 %collective-permute-start.16 = (bf16[2,64,1024]{2,1,0:T(8,128)(2,1)S(1)}, bf16[2,64,1024]{2,1,0:T(8,128)(2,1)S(1)}, u32[]{:S(2)}, u32[]{:S(2)}) collective-permute-start(bf16[2,64,1024]{2,1,0:T(8,128)(2,1)S(1)} %get-tuple-element.92), channel_id=1, source_target_pairs={{0,2},{1,3},{2,0},{3,1},{4,6},{5,7},{6,4},{7,5},{8,10},{9,11},{10,... | collective-permute-start | bytes 786440 | tf_op jit(solution)/shard_map/sum/ppermute | solution.py:612
  47.0 9.9 %collective-permute-start.11 = (bf16[64,1024]{1,0:T(8,128)(2,1)S(1)}, bf16[64,1024]{1,0:T(8,128)(2,1)S(1)}, u32[]{:S(2)}, u32[]{:S(2)}) collective-permute-start(bf16[64,1024]{1,0:T(8,128)(2,1)S(1)} %fusion.9), channel_id=1, source_target_pairs={{0,2},{1,3},{2,0},{3,1},{4,6},{5,7},{6,4},{7,5},{8,10},{9,11},{10,... | collective-permute-start | bytes 393224 | tf_op jit(solution)/shard_map/sum/ppermute | solution.py:612
  48.6 8.4 %collective-permute-start.13 = (bf16[64,1024]{1,0:T(8,128)(2,1)S(1)}, bf16[64,1024]{1,0:T(8,128)(2,1)S(1)}, u32[]{:S(2)}, u32[]{:S(2)}) collective-permute-start(bf16[64,1024]{1,0:T(8,128)(2,1)S(1)} %fusion.6), channel_id=1, source_target_pairs={{0,1},{1,0},{2,3},{3,2},{4,5},{5,4},{6,7},{7,6},{8,9},{9,8},{10,11... | collective-permute-start | bytes 393224 | tf_op jit(solution)/shard_map/sum/ppermute | solution.py:612
  52.6 6.0 %collective-permute-start.15 = (bf16[64,1024]{1,0:T(8,128)(2,1)S(1)}, bf16[64,1024]{1,0:T(8,128)(2,1)S(1)}, u32[]{:S(2)}, u32[]{:S(2)}) collective-permute-start(bf16[64,1024]{1,0:T(8,128)(2,1)S(1)} %fusion.3), channel_id=1, source_target_pairs={{0,2},{1,3},{2,0},{3,1},{4,6},{5,7},{6,4},{7,5},{8,10},{9,11},{10,... | collective-permute-start | bytes 393224 | tf_op jit(solution)/shard_map/sum/ppermute | solution.py:612
  54.3 5.0 %collective-permute-start.17 = (bf16[64,1024]{1,0:T(8,128)(2,1)S(1)}, bf16[64,1024]{1,0:T(8,128)(2,1)S(1)}, u32[]{:S(2)}, u32[]{:S(2)}) collective-permute-start(bf16[64,1024]{1,0:T(8,128)(2,1)S(1)} %fusion), channel_id=1, source_target_pairs={{0,1},{1,0},{2,3},{3,2},{4,5},{5,4},{6,7},{7,6},{8,9},{9,8},{10,11... | collective-permute-start | bytes 393224 | tf_op jit(solution)/shard_map/sum/ppermute | solution.py:612
